TPU v7x, 128 devices: a whole 4x4x4 slice. The times are simulated.
128 devices in a mesh: dp: 8 (over z, x_hi), mp: 16 (over y, x_lo, core).
Axes of the slice: x: 4 (x_hi: 2, x_lo: 2; x = x_hi * 2 + x_lo), y: 4, z: 4, core: 2. Of those that a mesh axis runs over, the one named last changes fastest.
Arguments:
- block_input_tokens: bfloat16 [6144, 3072], P(('dp', 'mp')), may hold values from -6 to 6
- norm_gain_vector: float32 [3072], replicated, may hold values from 0.5 to 1.5
- w_in: bfloat16 [3072, 24576], P(None, 'mp'), may hold values from -0.109375 to 0.109375
- w_out: bfloat16 [16384, 3072], P('mp'), may hold values from -0.046875 to 0.046875
- saved_qkv: bfloat16 [6144, 12288], P('dp', 'mp'), may hold values from -46 to 46
- mlp_pre: bfloat16 [6144, 12288], P('dp', 'mp'), may hold values from -6 to 6
- output_gradient: bfloat16 [6144, 3072], P(('dp', 'mp')), may hold values from -24 to 24
Outputs:
- input_gradient: bfloat16 [6144, 3072], P(('dp', 'mp'))
- grad_w_in: float32 [3072, 24576], P('dp', 'mp')
- grad_w_out: float32 [16384, 3072], P('mp', 'dp')
All inputs are finite; a program needn't handle non-finite values.
Results may differ from a plain program's by a relative error of at most 0.025.
Values may be sent and summed in bfloat16 or wider, within the bound.
A program may use at most 192 MiB of HBM per device.

v0:
```python
import jax
import jax.numpy as jnp
from jax import lax
from jax.sharding import PartitionSpec as P

HD = 128
HEADS_DEV = 2
PATCHES = 256


def layer_statistics(block_input_tokens):
    values = block_input_tokens.astype(jnp.float32)
    center = jnp.mean(values, axis=-1, keepdims=True)
    spread = jnp.mean((values - center) ** 2, axis=-1, keepdims=True)
    inverse_deviation = 1.0 / jnp.sqrt(spread + 1e-06)
    return ((values - center) * inverse_deviation, inverse_deviation)


def gelu_slope(pre):
    cumul = 0.5 * (1.0 + jax.scipy.special.erf(pre * 0.7071067811865476))
    dens = jnp.exp(-0.5 * pre * pre) * 0.3989422804014327
    return cumul + pre * dens


def contract_rows(left, right):
    return lax.dot_general(
        left, right, (((0,), (0,)), ((), ())), preferred_element_type=jnp.float32
    )


def contract_cols(left, right):
    return lax.dot_general(
        left, right, (((1,), (1,)), ((), ())), preferred_element_type=jnp.float32
    )


def body(block_input_tokens, norm_gain_vector, w_in, w_out, saved_qkv, mlp_pre, output_gradient):
    scale = HD ** (-0.5)
    att_cols = HEADS_DEV * HD
    group_rows = saved_qkv.shape[0]
    image_count = group_rows // PATCHES
    centered_standardized, inverse_deviation = layer_statistics(block_input_tokens)
    normalized_tokens = (centered_standardized * norm_gain_vector).astype(jnp.bfloat16)
    queries = saved_qkv[:, :att_cols].reshape(image_count, PATCHES, HEADS_DEV, HD)
    keys = saved_qkv[:, att_cols : 2 * att_cols].reshape(image_count, PATCHES, HEADS_DEV, HD)
    values = saved_qkv[:, 2 * att_cols :].reshape(image_count, PATCHES, HEADS_DEV, HD)
    scores = (
        jnp.einsum("bqhd,bkhd->bhqk", queries, keys, preferred_element_type=jnp.float32) * scale
    )
    probs_f = jax.nn.softmax(scores, axis=-1)
    probs = probs_f.astype(jnp.bfloat16)
    heads_out = jnp.einsum(
        "bhqk,bkhd->bqhd", probs, values, preferred_element_type=jnp.float32
    ).astype(jnp.bfloat16)
    pre = mlp_pre.astype(jnp.float32)
    act = jax.nn.gelu(pre, approximate=False).astype(jnp.bfloat16)
    joined = jnp.concatenate([heads_out.reshape(group_rows, att_cols), act], axis=1)
    piece = lax.all_gather(output_gradient, "mp", axis=0, tiled=True)
    part = contract_cols(piece, w_out)
    grad_acc = part
    grad_acc, local_w_out = (grad_acc, contract_rows(joined, piece))
    grad_joined = grad_acc.astype(jnp.bfloat16)
    grad_heads = grad_joined[:, :att_cols].reshape(image_count, PATCHES, HEADS_DEV, HD)
    grad_act = grad_joined[:, att_cols:]
    grad_v = jnp.einsum(
        "bhqk,bqhd->bkhd", probs, grad_heads, preferred_element_type=jnp.float32
    ).astype(jnp.bfloat16)
    grad_probs = jnp.einsum(
        "bqhd,bkhd->bhqk", grad_heads, values, preferred_element_type=jnp.float32
    )
    delta = jnp.sum(grad_heads.astype(jnp.float32) * heads_out.astype(jnp.float32), axis=-1)
    delta = jnp.transpose(delta, (0, 2, 1))[..., None]
    grad_scores = (probs_f * (grad_probs - delta) * scale).astype(jnp.bfloat16)
    grad_q = jnp.einsum(
        "bhqk,bkhd->bqhd", grad_scores, keys, preferred_element_type=jnp.float32
    ).astype(jnp.bfloat16)
    grad_k = jnp.einsum(
        "bhqk,bqhd->bkhd", grad_scores, queries, preferred_element_type=jnp.float32
    ).astype(jnp.bfloat16)
    grad_pre = (grad_act.astype(jnp.float32) * gelu_slope(pre)).astype(jnp.bfloat16)
    grad_proj = jnp.concatenate(
        [
            grad_q.reshape(group_rows, att_cols),
            grad_k.reshape(group_rows, att_cols),
            grad_v.reshape(group_rows, att_cols),
            grad_pre,
        ],
        axis=1,
    )
    local_w_in = contract_rows(
        lax.all_gather(normalized_tokens, "mp", axis=0, tiled=True), grad_proj
    )
    shard_w_out, shard_w_in = (
        lax.psum_scatter(
            local_w_out.astype(jnp.bfloat16), "dp", scatter_dimension=1, tiled=True
        ).astype(jnp.float32),
        lax.psum_scatter(
            local_w_in.astype(jnp.bfloat16), "dp", scatter_dimension=0, tiled=True
        ).astype(jnp.float32),
    )
    grad_normed = lax.psum_scatter(
        contract_cols(grad_proj, w_in).astype(jnp.bfloat16), "mp", scatter_dimension=0, tiled=True
    ).astype(jnp.float32)
    scaled_gradient = grad_normed * norm_gain_vector
    first_moment = jnp.mean(scaled_gradient, axis=-1, keepdims=True)
    second_moment = jnp.mean(scaled_gradient * centered_standardized, axis=-1, keepdims=True)
    input_gradient = (
        output_gradient.astype(jnp.float32)
        + (scaled_gradient - first_moment - centered_standardized * second_moment)
        * inverse_deviation
    )
    return (input_gradient.astype(jnp.bfloat16), shard_w_in, shard_w_out)


def solution(mesh):
    placed = (
        P(("dp", "mp"), None),
        P(),
        P(None, "mp"),
        P("mp", None),
        P("dp", "mp"),
        P("dp", "mp"),
        P(("dp", "mp"), None),
    )
    return jax.shard_map(
        body,
        mesh=mesh,
        in_specs=placed,
        out_specs=(P(("dp", "mp"), None), P("dp", "mp"), P("mp", "dp")),
        check_vma=False,
    )
```

profile of v0, /device:TPU:0, one launch (start us, length us, event | category | flops | bytes accessed | tf_op | source)
XLA Modules:
  0.0 439.6 jit_solution(16943360008900737109)
XLA Ops:
  7.2 0.7 all-gather.3.cloned.1.call-update
  7.9 1.3 fusion.82
  9.4 0.4 copy.45
  10.0 1.8 fusion.83
  11.8 39.0 %all-gather.3.cloned.1.call-done = bf16[768,3072]{1,0:T(8,128)(2,1)} async-done(((bf16[48,3072]{1,0:T(8,128)(2,1)}), bf16[768,3072]{1,0:T(8,128)(2,1)}) %all-gather.3.cloned.1.call-update) | async-done | bytes 4718608 | tf_op jit(solution)/shard_map/all_gather | solution.py:58
  50.8 8.6 %convolution_convert_fusion.3 = bf16[768,1024]{1,0:T(8,128)(2,1)S(1)} fusion(bf16[768,3072]{1,0:T(8,128)(2,1)} %all-gather.3.cloned.1.call-done, bf16[1024,3072]{1,0:T(8,128)(2,1)} %param.10), kind=kOutput, calls=%fused_computation.52 | convolution fusion | flops 4832624640 | bytes 12582912 | tf_op jit(solution)/shard_map/dot_general | solution.py:32
  59.5 0.4 copy.43
  60.0 2.7 fusion.47
  62.7 1.0 multiply_reduce_fusion
  63.7 0.4 multiply_convert_fusion
  64.5 0.4 fusion.45
  65.0 0.5 copy-done.2
  65.4 7.0 %fusion.3 = (bf16[768,768]{1,0:T(8,128)(2,1)}, bf16[768,768]{1,0:T(8,128)(2,1)}) fusion(bf16[768,768]{1,0:T(8,128)(2,1)S(1)} %copy-done.2, bf16[768,1024]{1,0:T(8,128)(2,1)S(1)} %convolution_convert_fusion.3), kind=kLoop, calls=%fused_computation.13 | loop fusion | flops 45416448 | bytes 4718592 | tf_op jit(solution)/shard_map/convert_element_type | solution.py:56
  72.5 1.4 copy.54
  73.9 0.4 copy.49
  74.3 0.4 copy.51
  74.9 0.7 copy-done.5
  75.8 12.7 %convolution_convert_fusion.2 = bf16[768,3072]{1,0:T(8,128)(2,1)} fusion(bf16[3072,1536]{1,0:T(8,128)(2,1)} %param.9, bf16[768,768]{1,0:T(8,128)(2,1)S(1)} %copy-done.3, bf16[768,256]{1,0:T(8,128)(2,1)S(1)} %get-tuple-element.16, bf16[768,256]{1,0:T(8,128)(2,1)S(1)} %get-tuple-element.17, bf16[768,256]{1,0:T(8,128)(2,1)S(1)} %bitcast.46), kind=kOutput, calls=%fused_computation.9 | convolution fusion | flops 7259553792 | bytes 16515072 | tf_op jit(solution)/shard_map/dot_general | solution.py:32
  88.6 0.9 copy-done
  89.9 69.4 %reduce-scatter.6.cloned.1.call-done = bf16[48,3072]{1,0:T(8,128)(2,1)} async-done(((bf16[768,3072]{1,0:T(8,128)(2,1)}), bf16[48,3072]{1,0:T(8,128)(2,1)}) %reduce-scatter.6.cloned.1.call-update) | async-done | bytes 294928 | tf_op jit(solution)/shard_map/reduce_scatter | solution.py:101
  159.3 1.2 fusion.62
  160.6 2.1 fusion.60
  162.9 1.3 copy.55
  164.3 9.4 %convolution_convert_fusion.1 = bf16[1024,3072]{1,0:T(8,128)(2,1)} fusion(bf16[768,3072]{1,0:T(8,128)(2,1)} %all-gather.3.cloned.1.call-done, bf16[768,768]{1,0:T(8,128)(2,1)S(1)} %copy-done.4, bf16[768,256]{1,0:T(8,128)(2,1)S(1)} %bitcast.48), kind=kOutput, calls=%fused_computation.2 | convolution fusion | flops 4838129664 | bytes 12582912 | tf_op jit(solution)/shard_map/dot_general | solution.py:26
  173.7 8.7 %copy.60 = bf16[1024,3072]{0,1:T(8,128)(2,1)} copy(bf16[1024,3072]{1,0:T(8,128)(2,1)} %convolution_convert_fusion.1) | data formatting | bytes 12582912
  182.5 17.9 %all-gather.5.cloned.1.call-done = bf16[768,3072]{1,0:T(8,128)(2,1)} async-done(((bf16[48,3072]{1,0:T(8,128)(2,1)}), bf16[768,3072]{1,0:T(8,128)(2,1)}) %all-gather.5.cloned.1.call-update) | async-done | bytes 4718608 | tf_op jit(solution)/shard_map/all_gather | solution.py:91
  200.4 12.5 %convolution_convert_fusion = bf16[3072,1536]{1,0:T(8,128)(2,1)} fusion(bf16[768,3072]{1,0:T(8,128)(2,1)} %all-gather.5.cloned.1.call-done, bf16[768,768]{1,0:T(8,128)(2,1)S(1)} %copy-done.3, bf16[768,256]{1,0:T(8,128)(2,1)S(1)} %copy-done.6, bf16[768,256]{1,0:T(8,128)(2,1)S(1)} %copy-done.8, bf16[768,256]{1,0:T(8,128)(2,1)S(1)} %bitcast.47), kind=kOutput, calls=%fused_computation.1 | convolution fusion | flops 7261913088 | bytes 16515072 | tf_op jit(solution)/shard_map/dot_general | solution.py:26
  212.9 90.0 %reduce-scatter.10.cloned.1.call-done = bf16[384,1024]{1,0:T(8,128)(2,1)} async-done(((bf16[3072,1024]{1,0:T(8,128)(2,1)}), bf16[384,1024]{1,0:T(8,128)(2,1)}) %reduce-scatter.10.cloned.1.call-update) | async-done | bytes 786448
  302.9 1.5 copy.61
  304.4 1.2 convert_element_type.107
  305.7 124.4 %reduce-scatter.8.cloned.1.call-done = bf16[384,1536]{1,0:T(8,128)(2,1)} async-done(((bf16[3072,1536]{1,0:T(8,128)(2,1)}), bf16[384,1536]{1,0:T(8,128)(2,1)}) %reduce-scatter.8.cloned.1.call-update) | async-done | bytes 1179664 | tf_op jit(solution)/shard_map/reduce_scatter | solution.py:97
  430.1 3.0 convert_element_type.104
  (43 shorter events, 2.1 us)
Async XLA Ops:
  7.2 43.6 %all-gather.3.cloned.1.call-start = ((), (), s32[]{:S(2)}) async-start(), calls=%async_computation.3 | async-start | bytes 5013504 | tf_op jit(solution)/shard_map/all_gather | solution.py:58
  7.9 151.4 %reduce-scatter.6.cloned.1.call-start = ((), (), s32[]{:S(2)}) async-start(), calls=%async_computation.4 | async-start | bytes 5013504 | tf_op jit(solution)/shard_map/reduce_scatter | solution.py:101
  60.0 2.7 copy-start.10
  64.2 1.3 copy-start.2
  72.5 3.3 copy-start.3
  74.9 0.8 copy-start.5
  74.9 0.9 copy-start.7
  88.5 1.0 copy-start
  88.5 70.8 %copy-start.9 = (f32[3072]{0:T(1024)S(1)}, f32[3072]{0:T(1024)}, u32[]{:S(2)}) copy-start(f32[3072]{0:T(1024)} %param.8) | copy-start | bytes 36868
  88.5 72.1 %copy-start.1 = (bf16[48,3072]{1,0:T(8,128)(2,1)S(1)}, bf16[48,3072]{1,0:T(8,128)(2,1)}, u32[]{:S(2)}) copy-start(bf16[48,3072]{1,0:T(8,128)(2,1)} %param.13) | copy-start | bytes 884740
  88.6 75.7 %copy-start.4 = (bf16[768,768]{1,0:T(8,128)(2,1)S(1)}, bf16[768,768]{1,0:T(8,128)(2,1)}, u32[]{:S(2)}) copy-start(bf16[768,768]{1,0:T(8,128)(2,1)} %get-tuple-element.5) | copy-start | bytes 3538948
  88.6 111.8 %all-gather.5.cloned.1.call-start = ((), (), s32[]{:S(2)}) async-start(), calls=%async_computation.5 | async-start | bytes 5013504 | tf_op jit(solution)/shard_map/all_gather | solution.py:91
  162.7 140.2 %reduce-scatter.10.cloned.1.call-start = ((), (), s32[]{:S(2)}) async-start(), calls=%async_computation.7 | async-start | bytes 7077888
  182.5 18.0 %copy-start.6 = (bf16[768,256]{1,0:T(8,128)(2,1)S(1)}, bf16[768,256]{1,0:T(8,128)(2,1)}, u32[]{:S(2)}) copy-start(bf16[768,256]{1,0:T(8,128)(2,1)} %copy-done.5) | copy-start | bytes 1179652
  182.5 18.0 %copy-start.8 = (bf16[768,256]{1,0:T(8,128)(2,1)S(1)}, bf16[768,256]{1,0:T(8,128)(2,1)}, u32[]{:S(2)}) copy-start(bf16[768,256]{1,0:T(8,128)(2,1)} %copy-done.7) | copy-start | bytes 1179652
  182.5 247.6 %reduce-scatter.8.cloned.1.call-start = ((), (), s32[]{:S(2)}) async-start(), calls=%async_computation.6 | async-start | bytes 10616832 | tf_op jit(solution)/shard_map/reduce_scatter | solution.py:97
Sparse Core Ops, SparseCore 0:
  9.7 41.0 all-gather.2
  88.7 70.6 reduce-scatter.5
  162.8 37.5 all-gather.4
  204.1 98.7 reduce-scatter.9
  306.6 123.4 reduce-scatter.7
where the time goes:
time: 440 us
  waiting for transfers between devices  341 us (78%)
  matrix products  50 us (11%)
  local copies, waits for them, and re-layouts  18.8 us (4%)
  other arithmetic  15 us (3%)
  between operations  14 us (3%)
    reduce_scatter x1, waiting for transfers between devices, body(): lax.psum_scatter(local_w_in.astype(jnp.bfloat16), 'dp', scatter_dimension...  124 us
    unnamed x6, waiting for transfers between devices  90.8 us
    reduce_scatter x1, waiting for transfers between devices, body(): lax.psum_scatter(contract_cols(grad_proj, w_in).astype(jnp.bfloat16), 'mp...  69.4 us
    all_gather x1, waiting for transfers between devices, body(): piece = lax.all_gather(output_gradient, 'mp', axis=0, tiled=True)  39 us
    dot_general x2, matrix products, contract_rows(): lax.dot_general(left, right, (((0,), (0,)), ((), ())), preferred_element_...  21.9 us
    dot_general x2, matrix products, contract_cols(): lax.dot_general(left, right, (((1,), (1,)), ((), ())), preferred_element_...  21.3 us
    all_gather x1, waiting for transfers between devices, body(): lax.all_gather(normalized_tokens, 'mp', axis=0, tiled=True)  17.9 us
    unnamed x26, local copies, waits for them, and re-layouts  12.6 us
  transfers between devices with their start and end apart: 5, of which 5 were waited for; matrix products, arithmetic and copies ran while one was open for 9% of the time, Pallas kernels for 0%

commit v1 on v0

v1 whole, which is shorter than its diff:
```python
import functools

import jax
import jax.numpy as jnp
from jax import lax
from jax.experimental import pallas as pl
from jax.experimental.pallas import tpu as pltpu
from jax.sharding import PartitionSpec as P

HD = 128
F32 = jnp.float32
BF16 = jnp.bfloat16
SCALE = HD ** (-0.5)
MESH = pl.DeviceIdType.MESH
NSO = 2
NSI = 4
HO = 1024 // NSO // 2
HI = 384 // NSI // 2


def nt(a, b):
    return lax.dot_general(a, b, (((1,), (1,)), ((), ())), preferred_element_type=F32)


def nn(a, b):
    return lax.dot_general(a, b, (((1,), (0,)), ((), ())), preferred_element_type=F32)


def tn(a, b):
    return lax.dot_general(a, b, (((0,), (0,)), ((), ())), preferred_element_type=F32)


def loop(n, fn):
    def step(i, carry):
        fn(i)
        return carry

    lax.fori_loop(0, n, step, 0)


def al(v, m):
    return pl.multiple_of(v, m)


def kernel(
    tok, gain, win, wout, qkv_hbm, pre_hbm, dout,
    ig, gwin, gwout,
    buf_a, buf_b, qkv, pre, slope, pf, heads, joined_t, gh, gproj, wslot, cout, cin,
    rzo, rzi, rxo, rxi, rs_sib, rs_y, rs_x, ss_x, xhat, gn, own_tok, own_dout, rstd_ref,
    lsem, ag_s, ag_r, zo_s, zo_r, zi_s, zi_r, xo_s, xo_r, xi_s, xi_r, ms_s, ms_r,
    my_s, my_r, mx_s, mx_r,
):
    dp = lax.axis_index("dp")
    mp = lax.axis_index("mp")
    z = dp // 2
    xh = dp % 2
    y = mp // 4
    xl = (mp // 2) % 2
    c = mp % 2
    zp, zm, z2 = (z + 1) % 4, (z + 3) % 4, (z + 2) % 4
    yp, ym, y2 = (y + 1) % 4, (y + 3) % 4, (y + 2) % 4
    xn, cn, xo = 1 - xl, 1 - c, 1 - xh

    def m_of(yy, xx, cc):
        return yy * 4 + xx * 2 + cc

    d_sib = (dp, m_of(y, xl, cn))
    d_xn = (dp, m_of(y, xn, c))
    d_yp = (dp, m_of(yp, xl, c))
    d_ym = (dp, m_of(ym, xl, c))
    d_y2 = (dp, m_of(y2, xl, c))
    d_zp = (zp * 2 + xh, mp)
    d_zm = (zm * 2 + xh, mp)
    d_xo = (z * 2 + xo, mp)
    friends = (d_sib, d_xn, d_yp, d_ym, d_y2, d_zp, d_zm, d_xo)

    def load(src, dst, i):
        return pltpu.make_async_copy(src, dst, lsem.at[i])

    l_dout = load(dout, own_dout, 0)
    l_tok = load(tok, own_tok, 1)
    l_qkv = load(qkv_hbm, qkv, 2)
    l_pre = load(pre_hbm, pre, 3)
    for l in (l_dout, l_tok, l_qkv, l_pre):
        l.start()

    def wout_loads(nb, row):
        return [
            load(
                wout.at[pl.ds(nb * 256, 256), pl.ds(h * 1536, 1536)],
                wslot.at[pl.ds(row + h * 256, 256)],
                4 + nb * 2 + h,
            )
            for h in range(2)
        ]

    wo_rows = (0, 512, 1024, 0)
    wo_loads = [wout_loads(nb, wo_rows[nb]) for nb in range(4)]
    for nb in range(3):
        for l in wo_loads[nb]:
            l.start()

    barrier = pltpu.get_barrier_semaphore()
    for d in friends:
        pl.semaphore_signal(barrier, inc=1, device_id=d, device_id_type=MESH)
    pl.semaphore_wait(barrier, len(friends))

    def remote(src, dst, s, r, d):
        return pltpu.make_async_remote_copy(
            src_ref=src, dst_ref=dst, send_sem=s, recv_sem=r, device_id=d, device_id_type=MESH
        )

    order = (z2, zp, zm, z)
    me = m_of(y, xl, c)
    mx = m_of(y, xn, c)
    ag_out = (
        (me, d_sib), (me, d_xn), (me, d_yp), (me, d_ym), (me, d_y2),
        (mx, d_yp), (mx, d_ym), (mx, d_y2), (mx, d_sib),
        (m_of(ym, xl, c), d_sib), (m_of(yp, xl, c), d_sib), (m_of(y2, xl, c), d_sib),
        (m_of(ym, xn, c), d_sib), (m_of(yp, xn, c), d_sib), (m_of(y2, xn, c), d_sib),
    )
    ag_in = (
        m_of(y, xl, cn), mx, m_of(ym, xl, c), m_of(yp, xl, c), m_of(y2, xl, c),
        m_of(ym, xn, c), m_of(yp, xn, c), m_of(y2, xn, c), m_of(y, xn, cn),
        m_of(ym, xl, cn), m_of(yp, xl, cn), m_of(y2, xl, cn),
        m_of(ym, xn, cn), m_of(yp, xn, cn), m_of(y2, xn, cn),
    )
    bufs = (buf_a, buf_b)

    def block(w, o, m):
        return bufs[w].at[order[o], pl.ds(al(m * 48, 16), 48), :]

    def ag_send(w, o, ts):
        for t in ts:
            m, d = ag_out[t]
            b = block(w, o, m)
            remote(b, b, ag_s.at[w, o, t], ag_r.at[w, o, t], d).start()

    def ag_wait(w, o, ts):
        for t in ts:
            b = block(w, o, ag_in[t])
            remote(b, b, ag_s.at[w, o, t], ag_r.at[w, o, t], ag_out[t][1]).wait_recv()

    def ag_start(w, o):
        ag_send(w, o, (1, 2, 3, 4, 0))

    def ag_x(w, o):
        ag_wait(w, o, (1,))
        ag_send(w, o, (5, 6, 7, 8))

    def ag_y(w, o):
        ag_wait(w, o, (2, 3, 4))
        ag_send(w, o, (9, 10, 11))

    def ag_yx(w, o):
        ag_wait(w, o, (5, 6, 7))
        ag_send(w, o, (12, 13, 14))

    def ag_sib(w, o):
        ag_wait(w, o, (0, 8, 9, 10, 11, 12, 13, 14))

    def ag_drain(w):
        for o in range(4):
            for t in range(15):
                m, d = ag_out[t]
                b = block(w, o, m)
                remote(b, b, ag_s.at[w, o, t], ag_r.at[w, o, t], d).wait_send()

    l_dout.wait()
    for o in range(4):
        buf_a[order[o], pl.ds(al(me * 48, 16), 48), :] = own_dout[
            :, pl.ds(al(order[o] * 768, 128), 768)
        ]
        if o < 2:
            ag_start(0, o)

    l_tok.wait()
    x = own_tok[...].astype(F32)
    center = jnp.mean(x, axis=-1, keepdims=True)
    spread = jnp.mean((x - center) ** 2, axis=-1, keepdims=True)
    rstd = 1.0 / jnp.sqrt(spread + 1e-06)
    xhat[...] = (x - center) * rstd
    rstd_ref[...] = jnp.broadcast_to(rstd, rstd_ref.shape)
    for o in range(4):
        buf_b[o, pl.ds(al(me * 48, 16), 48), :] = (
            xhat[:, pl.ds(o * 768, 768)] * gain[:, pl.ds(o * 768, 768)]
        ).astype(BF16)

    def att_fwd(b):
        rows = pl.ds(b * 256, 256)
        for h in range(2):
            q = qkv[rows, pl.ds(h * 128, 128)]
            k = qkv[rows, pl.ds(256 + h * 128, 128)]
            v = qkv[rows, pl.ds(512 + h * 128, 128)]
            s = nt(q, k) * SCALE
            e = jnp.exp(s - jnp.max(s, axis=-1, keepdims=True))
            p = e / jnp.sum(e, axis=-1, keepdims=True)
            pf[b * 2 + h] = p
            out = nn(p.astype(BF16), v)
            heads[rows, pl.ds(h * 128, 128)] = out.astype(BF16)
            joined_t[pl.ds(h * 128, 128), rows] = jnp.transpose(out).astype(BF16)

    def gelu(t):
        rows = pl.ds(al(t * 128, 128), 128)
        v = pre[rows, :].astype(F32)
        cumul = 0.5 * (1.0 + lax.erf(v * 0.7071067811865476))
        joined_t[pl.ds(256, 768), rows] = jnp.transpose(v * cumul).astype(BF16)
        dens = jnp.exp(-0.5 * v * v) * 0.3989422804014327
        slope[rows, :] = cumul + v * dens

    l_qkv.wait()
    att_fwd(0)
    ag_x(0, 0)
    ag_start(0, 2)
    att_fwd(1)
    ag_x(0, 1)
    ag_start(0, 3)
    att_fwd(2)
    ag_y(0, 0)
    ag_x(0, 2)
    l_pre.wait()
    gelu(0)
    gelu(1)
    ag_yx(0, 0)
    ag_x(0, 3)
    gelu(2)
    gelu(3)
    ag_y(0, 1)
    ag_yx(0, 1)
    gelu(4)
    gelu(5)
    ag_sib(0, 0)
    ag_y(0, 2)

    class Ring:
        def __init__(self, src, rbuf, ssem, rsem, add):
            self.src, self.rbuf, self.ssem, self.rsem, self.add = src, rbuf, ssem, rsem, add
            self.sent = []

        def send(self, i, src, d):
            cp = remote(src, self.rbuf.at[i], self.ssem.at[i], self.rsem.at[i], d)
            cp.start()
            self.sent.append(cp)

        def wait(self, i):
            b = self.rbuf.at[i]
            remote(b, b, self.ssem.at[i], self.rsem.at[i], d_zp).wait_recv()

        def far(self):
            self.send(0, self.src(z2, 1), d_zp)
            self.send(1, self.src(z2, 0), d_zm)

        def near_p(self):
            self.send(2, self.src(zp, 0), d_zp)

        def near_m(self):
            self.send(3, self.src(zm, 1), d_zm)

        def relay_p(self):
            self.wait(0)
            self.add(self.rbuf.at[0], self.src(zp, 1))
            self.send(4, self.rbuf.at[0], d_zp)

        def relay_m(self):
            self.wait(1)
            self.add(self.rbuf.at[1], self.src(zm, 0))
            self.send(5, self.rbuf.at[1], d_zm)

        def arrived(self):
            for i in (2, 3, 4, 5):
                self.wait(i)

        def drain(self):
            for cp in self.sent:
                cp.wait_send()

    def add_o(dst, src):
        def step(i):
            rows = pl.ds(al(i * 64, 64), 64)
            for h in range(2):
                dst[h, rows, :] = (
                    dst[h, rows, :].astype(F32) + src[h, rows, :].astype(F32)
                ).astype(BF16)

        loop(HO // 64, step)

    def add_i(dst, src):
        def step(i):
            rows = pl.ds(al(i * 16, 16), 16)
            for h in range(2):
                dst[h, rows, :] = (
                    dst[h, rows, :].astype(F32) + src[h, rows, :].astype(F32)
                ).astype(BF16)

        loop(HI // 16, step)

    def src_o(s):
        return lambda zz, half: cout.at[
            pl.ds(zz * 2, 2), pl.ds(s * 2 * HO + half * HO, HO), :
        ]

    def src_i(s):
        return lambda zz, half: cin.at[
            pl.ds(zz * 2, 2), pl.ds(s * 2 * HI + half * HI, HI), :
        ]

    ro = [Ring(src_o(s), rzo.at[s], zo_s.at[s], zo_r.at[s], add_o) for s in range(NSO)]
    ri = [Ring(src_i(s), rzi.at[s], zi_s.at[s], zi_r.at[s], add_i) for s in range(NSI)]

    class Cross:
        def __init__(self, ring, part, rx, out, ssem, rsem, base, height, tile):
            self.ring, self.part, self.rx, self.out = ring, part, rx, out
            self.ssem, self.rsem = ssem, rsem
            self.base, self.height, self.tile = base, height, tile
            self.sent = []

        def send(self):
            self.ring.arrived()
            r = self.ring.rbuf
            for half, (a, b) in enumerate(((2, 5), (3, 4))):
                off = self.base + half * self.height

                def step(i, a=a, b=b, off=off):
                    rows = pl.ds(al(i * self.tile, self.tile), self.tile)
                    prow = pl.ds(al(off + i * self.tile, self.tile), self.tile)
                    r[a, xo, rows, :] = (
                        r[a, xo, rows, :].astype(F32)
                        + r[b, xo, rows, :].astype(F32)
                        + self.part[z * 2 + xo, prow, :].astype(F32)
                    ).astype(BF16)

                loop(self.height // self.tile, step)
                cp = remote(
                    r.at[a, xo], self.rx.at[pl.ds(off, self.height), :],
                    self.ssem.at[half], self.rsem.at[half], d_xo,
                )
                cp.start()
                self.sent.append(cp)

        def finish(self):
            r = self.ring.rbuf
            for half, (a, b) in enumerate(((2, 5), (3, 4))):
                off = self.base + half * self.height
                dst = self.rx.at[pl.ds(off, self.height), :]
                remote(dst, dst, self.ssem.at[half], self.rsem.at[half], d_xo).wait_recv()

                def step(i, a=a, b=b, off=off):
                    rows = pl.ds(al(i * self.tile, self.tile), self.tile)
                    prow = pl.ds(al(off + i * self.tile, self.tile), self.tile)
                    self.rx[prow, :] = (
                        r[a, xh, rows, :].astype(F32)
                        + r[b, xh, rows, :].astype(F32)
                        + self.part[z * 2 + xh, prow, :].astype(F32)
                        + self.rx[prow, :].astype(F32)
                    ).astype(BF16)

                loop(self.height // self.tile, step)

        def drain(self):
            for cp in self.sent:
                cp.wait_send()

    co = [
        Cross(ro[s], cout, rxo, gwout, xo_s.at[s], xo_r.at[s], s * 2 * HO, HO, 64)
        for s in range(NSO)
    ]
    ci = [
        Cross(ri[s], cin, rxi, gwin, xi_s.at[s], xi_r.at[s], s * 2 * HI, HI, 16)
        for s in range(NSI)
    ]

    def out_chunk(o):
        j = order[o]

        def step(r):
            rows = pl.ds(al(r * 256, 256), 256)
            t = nn(joined_t[rows, :], buf_a[j]).astype(BF16)
            cout[j * 2, rows, :] = t[:, :384]
            cout[j * 2 + 1, rows, :] = t[:, 384:]

        loop(4, step)

    out_chunk(0)
    for r in ro:
        r.far()
    ag_yx(0, 2)
    ag_sib(0, 1)
    ag_y(0, 3)
    out_chunk(1)
    for r in ro:
        r.near_p()
    ag_yx(0, 3)
    ag_sib(0, 2)
    out_chunk(2)
    for r in ro:
        r.near_m()
    ag_start(1, 0)
    ag_start(1, 1)
    ag_sib(0, 3)
    out_chunk(3)
    ag_x(1, 0)
    ag_x(1, 1)
    ag_start(1, 2)
    ag_start(1, 3)

    def joined_grad(nb):
        for l in wo_loads[nb]:
            l.wait()
        row = wo_rows[nb]

        def step(r):
            rows = pl.ds(al(r * 384, 128), 384)
            acc = jnp.zeros((384, 256), F32)
            for j in range(4):
                w = wslot[pl.ds(row + (j // 2) * 256, 256), pl.ds((j % 2) * 768, 768)]
                acc = acc + nt(buf_a[j, rows, :], w)
            g = acc.astype(BF16)
            if nb == 0:
                gh[rows, :] = g
            else:
                cols = pl.ds((nb - 1) * 256, 256)
                gproj[rows, pl.ds(768 + (nb - 1) * 256, 256)] = (
                    g.astype(F32) * slope[rows, cols]
                ).astype(BF16)

        loop(2, step)

    joined_grad(0)
    for l in wo_loads[3]:
        l.start()
    ro[0].relay_p()
    ro[0].relay_m()
    ag_x(1, 2)
    ag_x(1, 3)
    joined_grad(1)
    ag_y(1, 0)
    ag_y(1, 1)
    joined_grad(2)
    ag_yx(1, 0)
    ag_yx(1, 1)
    joined_grad(3)
    ag_y(1, 2)
    ag_y(1, 3)
    ro[1].relay_p()
    ro[1].relay_m()

    def win_load(j):
        return load(
            win.at[pl.ds(j * 768, 768), :], wslot.at[pl.ds((j % 2) * 768, 768)], 12 + j
        )

    win_load(0).start()
    win_load(1).start()

    def att_bwd(b):
        rows = pl.ds(b * 256, 256)
        for h in range(2):
            q = qkv[rows, pl.ds(h * 128, 128)]
            k = qkv[rows, pl.ds(256 + h * 128, 128)]
            v = qkv[rows, pl.ds(512 + h * 128, 128)]
            g = gh[rows, pl.ds(h * 128, 128)]
            p = pf[b * 2 + h]
            delta = jnp.sum(
                g.astype(F32) * heads[rows, pl.ds(h * 128, 128)].astype(F32),
                axis=-1, keepdims=True,
            )
            ds = (p * (nt(g, v) - delta) * SCALE).astype(BF16)
            gproj[rows, pl.ds(512 + h * 128, 128)] = tn(p.astype(BF16), g).astype(BF16)
            gproj[rows, pl.ds(h * 128, 128)] = nn(ds, k).astype(BF16)
            gproj[rows, pl.ds(256 + h * 128, 128)] = tn(ds, q).astype(BF16)

    att_bwd(0)
    ag_yx(1, 2)
    ag_yx(1, 3)
    att_bwd(1)
    att_bwd(2)

    ag_drain(0)

    def transposed(o):
        ag_sib(1, o)
        j = order[o]

        def step(i):
            rows = pl.ds(al(i * 128, 128), 128)
            buf_a[j, :, rows] = jnp.transpose(buf_b[j, rows, :])

        loop(6, step)

    def in_chunk(o):
        j = order[o]

        def step(i):
            h, n = i // 2, i % 2
            rows = pl.ds(al(h * 384, 128), 384)
            cols = pl.ds(al(n * 768, 128), 768)
            cin[j * 2 + h, :, cols] = nn(buf_a[j, rows, :], gproj[:, cols]).astype(BF16)

        loop(4, step)

    transposed(0)
    in_chunk(0)
    for r in ri:
        r.far()
    transposed(1)
    in_chunk(1)
    for r in ri:
        r.near_p()
    transposed(2)
    in_chunk(2)
    for r in ri:
        r.near_m()
    transposed(3)
    in_chunk(3)
    co[0].send()
    co[1].send()
    ag_drain(1)

    def sib_copy(j):
        return remote(
            buf_b.at[j, pl.ds(al(cn * 384, 128), 384), :], rs_sib.at[j],
            ms_s.at[j], ms_r.at[j], d_sib,
        )

    def normed_grad(j):
        win_load(j).wait()
        base = (j % 2) * 768

        def step(i):
            h, n = i // 3, i % 3
            rows = pl.ds(al(h * 384, 128), 384)
            w = wslot[pl.ds(al(base + n * 256, 256), 256), :]
            t = nt(gproj[rows, :], w).astype(BF16)
            cols = pl.ds(al(n * 256, 128), 256)
            for b in range(8):
                buf_b[j, pl.ds(al((b % 2) * 384 + (h * 4 + b // 2) * 48, 16), 48), cols] = t[
                    b * 48 : b * 48 + 48
                ]

        loop(6, step)
        sib_copy(j).start()
        if j < 2:
            win_load(j + 2).start()

    y_rows = {0: yp, 1: ym, 2: y2}
    y_dev = (d_yp, d_ym, d_y2)

    def y_copy(j, i):
        return remote(
            buf_b.at[j, pl.ds(al(c * 384 + y_rows[i] * 96, 16), 96), :], rs_y.at[i, j],
            my_s.at[i, j], my_r.at[i, j], y_dev[i],
        )

    def sib_sum(j):
        sib_copy(j).wait_recv()

        def step(i):
            rows = pl.ds(al(c * 384 + i * 48, 16), 48)
            buf_b[j, rows, :] = (
                buf_b[j, rows, :].astype(F32)
                + rs_sib[j, pl.ds(al(i * 48, 16), 48), :].astype(F32)
            ).astype(BF16)

        loop(8, step)
        for i in range(3):
            y_copy(j, i).start()

    def x_copy(j):
        return remote(ss_x.at[j], rs_x.at[j], mx_s.at[j], mx_r.at[j], d_xn)

    def y_sum(j):
        for i in range(3):
            y_copy(j, i).wait_recv()

        def total(side):
            acc = buf_b[j, pl.ds(al(c * 384 + y * 96 + side * 48, 16), 48), :].astype(F32)
            for i in range(3):
                acc = acc + rs_y[i, j, pl.ds(al(side * 48, 16), 48), :].astype(F32)
            return acc

        ss_x[j] = total(xn).astype(BF16)
        x_copy(j).start()
        gn[:, pl.ds(j * 768, 768)] = total(xl)

    def x_sum(j):
        x_copy(j).wait_recv()
        cols = pl.ds(j * 768, 768)
        gn[:, cols] = gn[:, cols] + rs_x[j].astype(F32)

    normed_grad(0)
    ri[0].relay_p()
    ri[0].relay_m()
    normed_grad(1)
    sib_sum(0)
    normed_grad(2)
    sib_sum(1)
    ri[1].relay_p()
    ri[1].relay_m()
    normed_grad(3)
    sib_sum(2)
    co[0].finish()
    co[1].finish()
    st_o = load(rxo, gwout, 0)
    st_o.start()
    sib_sum(3)
    y_sum(0)
    ri[2].relay_p()
    ri[2].relay_m()
    y_sum(1)
    y_sum(2)
    y_sum(3)
    ri[3].relay_p()
    ri[3].relay_m()
    for j in range(4):
        x_sum(j)
    xh_v = xhat[...]
    sg = gn[...] * gain[...]
    m1 = jnp.mean(sg, axis=-1, keepdims=True)
    m2 = jnp.mean(sg * xh_v, axis=-1, keepdims=True)
    own_tok[...] = (
        own_dout[...].astype(F32) + (sg - m1 - xh_v * m2) * rstd_ref[:, :1]
    ).astype(BF16)
    st_g = load(own_tok, ig, 1)
    st_g.start()
    for s in range(NSI):
        ci[s].send()
    for s in range(NSI):
        ci[s].finish()
    st_i = load(rxi, gwin, 2)
    st_i.start()
    for r in ro + ri + co + ci:
        r.drain()
    for j in range(4):
        sib_copy(j).wait_send()
        x_copy(j).wait_send()
        for i in range(3):
            y_copy(j, i).wait_send()
    st_o.wait()
    st_g.wait()
    st_i.wait()


def body(block_input_tokens, norm_gain_vector, w_in, w_out, saved_qkv, mlp_pre, output_gradient):
    hbm = pl.BlockSpec(memory_space=pl.ANY)
    vmem = pl.BlockSpec(memory_space=pltpu.VMEM)
    sem = pltpu.SemaphoreType.DMA
    v = pltpu.VMEM
    ig, gwin, gwout = pl.pallas_call(
        kernel,
        name="block_backward",
        out_shape=(
            jax.ShapeDtypeStruct((48, 3072), BF16),
            jax.ShapeDtypeStruct((384, 1536), BF16),
            jax.ShapeDtypeStruct((1024, 384), BF16),
        ),
        in_specs=[hbm, vmem, hbm, hbm, hbm, hbm, hbm],
        out_specs=(hbm, hbm, hbm),
        scratch_shapes=[
            v((4, 768, 768), BF16), v((4, 768, 768), BF16), v((768, 768), BF16),
            v((768, 768), BF16), v((768, 768), F32), v((6, 256, 256), F32),
            v((768, 256), BF16), v((1024, 768), BF16), v((768, 256), BF16),
            v((768, 1536), BF16), v((1536, 1536), BF16), v((8, 1024, 384), BF16),
            v((8, 384, 1536), BF16),
            v((NSO, 6, 2, HO, 384), BF16), v((NSI, 6, 2, HI, 1536), BF16),
            v((1024, 384), BF16), v((384, 1536), BF16), v((4, 384, 768), BF16),
            v((3, 4, 96, 768), BF16), v((4, 48, 768), BF16), v((4, 48, 768), BF16),
            v((48, 3072), F32), v((48, 3072), F32), v((48, 3072), BF16),
            v((48, 3072), BF16), v((48, 128), F32),
            sem((16,)), sem((2, 4, 15)), sem((2, 4, 15)),
            sem((NSO, 6)), sem((NSO, 6)), sem((NSI, 6)), sem((NSI, 6)),
            sem((NSO, 2)), sem((NSO, 2)), sem((NSI, 2)), sem((NSI, 2)),
            sem((4,)), sem((4,)), sem((3, 4)), sem((3, 4)), sem((4,)), sem((4,)),
        ],
        compiler_params=pltpu.CompilerParams(
            collective_id=0, has_side_effects=True, vmem_limit_bytes=63 << 20
        ),
    )(
        block_input_tokens, norm_gain_vector.reshape(1, -1), w_in, w_out, saved_qkv, mlp_pre,
        output_gradient,
    )
    return ig, gwin.astype(F32), gwout.astype(F32)


def solution(mesh):
    placed = (
        P(("dp", "mp"), None),
        P(),
        P(None, "mp"),
        P("mp", None),
        P("dp", "mp"),
        P("dp", "mp"),
        P(("dp", "mp"), None),
    )
    return jax.shard_map(
        body,
        mesh=mesh,
        in_specs=placed,
        out_specs=(P(("dp", "mp"), None), P("dp", "mp"), P("mp", "dp")),
        check_vma=False,
    )
```

time: 440 us -> 175 us (0.40)
  waiting for transfers between devices: 341 us -> 0 us
  Pallas kernels: 0 us -> 169 us
  matrix products: 50 us -> 0 us
  local copies, waits for them, and re-layouts: 18.8 us -> 0.72 us
  between operations: 14 us -> 0.65 us
  other arithmetic: 15 us -> 4.28 us
    reduce_scatter x2 -> x0, waiting for transfers between devices: 194 us -> none  [the longest x1 124 us: body(): lax.psum_scatter(local_w_in.astype(jnp.bfloat16), 'dp', scatter_dimension...]
    pallas_call x0 -> x1, Pallas kernels: none -> 169 us  [body(): pl.pallas_call(kernel, name='block_backward', out_shape=(jax.ShapeDtypeSt...]
    unnamed x6 -> x0, waiting for transfers between devices: 90.8 us -> none
    all_gather x2 -> x0, waiting for transfers between devices: 56.9 us -> none  [the longest x1 39 us: body(): piece = lax.all_gather(output_gradient, 'mp', axis=0, tiled=True)]
    dot_general x9 -> x0, matrix products: 48.2 us -> none  [the longest x2 21.9 us: contract_rows(): lax.dot_general(left, right, (((0,), (0,)), ((), ())), preferred_element_...]
    unnamed x26 -> x5, local copies, waits for them, and re-layouts: 12.6 us -> 0.72 us
    convert_element_type x4 -> x2, other arithmetic: 13.3 us -> 4.28 us  [body(): return (ig, gwin.astype(F32), gwout.astype(F32))]
  transfers between devices with their start and end apart: 5 -> 0, of which waited for: 5 -> 0; matrix products, arithmetic and copies ran while one was open for 9% -> 0% of each run, Pallas kernels for 0% -> 0%
where the time goes in v1:
time: 175 us
  Pallas kernels  169 us (97%)
  other arithmetic  4.28 us (2%)
    pallas_call x1, Pallas kernels, body(): pl.pallas_call(kernel, name='block_backward', out_shape=(jax.ShapeDtypeSt...  169 us
    convert_element_type x2, other arithmetic, body(): return (ig, gwin.astype(F32), gwout.astype(F32))  4.28 us

profile of v1, /device:TPU:0, one launch (start us, length us, event | category | flops | bytes accessed | tf_op | source)
XLA Modules:
  0.0 174.6 jit_solution(7920655460257247447)
XLA Ops:
  0.6 168.9 %block_backward.1 = (bf16[48,3072]{1,0:T(8,128)(2,1)}, bf16[384,1536]{1,0:T(8,128)(2,1)}, bf16[1024,384]{1,0:T(8,128)(2,1)}) custom-call(bf16[48,3072]{1,0:T(8,128)(2,1)} %tok.1, f32[1,3072]{1,0:T(1,128)} %bitcast.1, bf16[3072,1536]{1,0:T(8,128)(2,1)} %win.1, bf16[1024,3072]{1,0:T(8,128)(2,1)} %wout.1, bf16[768,768]{1,0:T(8,128)(2,1)} %qkv_hbm.1, ...), custom_call_target="tpu_custom_call" | custom-call | tf_op jit(solution)/shard_map/block_backward/pallas_call | solution.py:648
  169.6 0.0 copy-start
  169.6 3.0 %convert_element_type.6 = f32[384,1536]{1,0:T(8,128)} convert(bf16[384,1536]{1,0:T(8,128)(2,1)} %get-tuple-element.7) | non-fusion elementwise | flops 589824 | bytes 3538944 | tf_op jit(solution)/shard_map/convert_element_type | solution.py:681
  172.6 0.0 copy-start.1
  172.6 0.0 copy-done
  172.6 1.2 convert_element_type.7
  173.9 0.0 copy-done.1
  173.9 0.7 copy.11
Async XLA Ops:
  169.6 3.1 %copy-start = (bf16[1024,384]{1,0:T(8,128)(2,1)S(1)}, bf16[1024,384]{1,0:T(8,128)(2,1)}, u32[]{:S(2)}) copy-start(bf16[1024,384]{1,0:T(8,128)(2,1)} %get-tuple-element.8) | copy-start | bytes 2359300
  172.6 1.3 copy-start.1

commit v2 on v1

--- a/solution.py
+++ b/solution.py
@@ -12,10 +12,8 @@
 BF16 = jnp.bfloat16
 SCALE = HD ** (-0.5)
 MESH = pl.DeviceIdType.MESH
-NSO = 2
-NSI = 4
-HO = 1024 // NSO // 2
-HI = 384 // NSI // 2
+NSO, HO, XO = 2, 128, 512
+NSI, HI, XI = 3, 48, 96
 
 
 def nt(a, b):
@@ -46,9 +44,9 @@
     tok, gain, win, wout, qkv_hbm, pre_hbm, dout,
     ig, gwin, gwout,
     buf_a, buf_b, qkv, pre, slope, pf, heads, joined_t, gh, gproj, wslot, cout, cin,
-    rzo, rzi, rxo, rxi, rs_sib, rs_y, rs_x, ss_x, xhat, gn, own_tok, own_dout, rstd_ref,
-    lsem, ag_s, ag_r, zo_s, zo_r, zi_s, zi_r, xo_s, xo_r, xi_s, xi_r, ms_s, ms_r,
-    my_s, my_r, mx_s, mx_r,
+    rzo, rzi, rfo, rfi, x1o, x1i, rxo, rxi, rs_sib, rs_y, rs_x, ss_x, xhat, gn, own_tok, own_dout, rstd_ref,
+    lsem, ag_s, ag_r, zo_s, zo_r, zi_s, zi_r, fo_s, fo_r, fi_s, fi_r, xo_s, xo_r, xi_s, xi_r,
+    x1o_s, x1o_r, x1i_s, x1i_r, ms_s, ms_r, my_s, my_r, mx_s, mx_r,
 ):
     dp = lax.axis_index("dp")
     mp = lax.axis_index("mp")
@@ -113,66 +111,78 @@
     order = (z2, zp, zm, z)
     me = m_of(y, xl, c)
     mx = m_of(y, xn, c)
+    b_ym, b_yp, b_y2 = m_of(ym, xl, c), m_of(yp, xl, c), m_of(y2, xl, c)
+    b_xym, b_xyp, b_xy2 = m_of(ym, xn, c), m_of(yp, xn, c), m_of(y2, xn, c)
     ag_out = (
-        (me, d_sib), (me, d_xn), (me, d_yp), (me, d_ym), (me, d_y2),
-        (mx, d_yp), (mx, d_ym), (mx, d_y2), (mx, d_sib),
-        (m_of(ym, xl, c), d_sib), (m_of(yp, xl, c), d_sib), (m_of(y2, xl, c), d_sib),
-        (m_of(ym, xn, c), d_sib), (m_of(yp, xn, c), d_sib), (m_of(y2, xn, c), d_sib),
+        (me, 0, d_sib), (me, 0, d_xn), (me, 0, d_yp), (me, 0, d_ym),
+        (mx, 0, d_yp), (mx, 0, d_ym), (mx, 0, d_sib),
+        (b_ym, 1, d_yp), (b_yp, 2, d_ym), (b_ym, 0, d_sib), (b_yp, 0, d_sib),
+        (b_xym, 1, d_yp), (b_xyp, 2, d_ym), (b_xym, 0, d_sib), (b_xyp, 0, d_sib),
+        (b_y2, 0, d_sib), (b_xy2, 0, d_sib),
     )
     ag_in = (
-        m_of(y, xl, cn), mx, m_of(ym, xl, c), m_of(yp, xl, c), m_of(y2, xl, c),
-        m_of(ym, xn, c), m_of(yp, xn, c), m_of(y2, xn, c), m_of(y, xn, cn),
-        m_of(ym, xl, cn), m_of(yp, xl, cn), m_of(y2, xl, cn),
-        m_of(ym, xn, cn), m_of(yp, xn, cn), m_of(y2, xn, cn),
+        m_of(y, xl, cn), mx, b_ym, b_yp, b_xym, b_xyp, m_of(y, xn, cn),
+        b_y2, b_y2, m_of(ym, xl, cn), m_of(yp, xl, cn),
+        b_xy2, b_xy2, m_of(ym, xn, cn), m_of(yp, xn, cn), m_of(y2, xl, cn), m_of(y2, xn, cn),
     )
     bufs = (buf_a, buf_b)
 
-    def block(w, o, m):
-        return bufs[w].at[order[o], pl.ds(al(m * 48, 16), 48), :]
+    def block(w, o, m, part):
+        cols = (slice(None), pl.ds(0, 384), pl.ds(384, 384))[part]
+        return bufs[w].at[order[o], pl.ds(al(m * 48, 16), 48), cols]
+
+    def ag_copy(w, o, t, m):
+        b = block(w, o, m, ag_out[t][1])
+        return remote(b, b, ag_s.at[w, o, t], ag_r.at[w, o, t], ag_out[t][2])
 
     def ag_send(w, o, ts):
         for t in ts:
-            m, d = ag_out[t]
-            b = block(w, o, m)
-            remote(b, b, ag_s.at[w, o, t], ag_r.at[w, o, t], d).start()
+            ag_copy(w, o, t, ag_out[t][0]).start()
 
     def ag_wait(w, o, ts):
         for t in ts:
-            b = block(w, o, ag_in[t])
-            remote(b, b, ag_s.at[w, o, t], ag_r.at[w, o, t], ag_out[t][1]).wait_recv()
-
-    def ag_start(w, o):
-        ag_send(w, o, (1, 2, 3, 4, 0))
+            ag_copy(w, o, t, ag_in[t]).wait_recv()
+
+    def ag_sx(w, o):
+        ag_send(w, o, (1,))
+
+    def ag_sy(w, o):
+        ag_send(w, o, (2, 3, 0))
 
     def ag_x(w, o):
         ag_wait(w, o, (1,))
-        ag_send(w, o, (5, 6, 7, 8))
+        ag_send(w, o, (4, 5, 6))
 
     def ag_y(w, o):
-        ag_wait(w, o, (2, 3, 4))
-        ag_send(w, o, (9, 10, 11))
+        ag_wait(w, o, (2, 3))
+        ag_send(w, o, (7, 8, 9, 10))
 
     def ag_yx(w, o):
-        ag_wait(w, o, (5, 6, 7))
-        ag_send(w, o, (12, 13, 14))
+        ag_wait(w, o, (4, 5))
+        ag_send(w, o, (11, 12, 13, 14))
+
+    def ag_far(w, o):
+        ag_wait(w, o, (7, 8))
+        ag_send(w, o, (15,))
+        ag_wait(w, o, (11, 12))
+        ag_send(w, o, (16,))
 
     def ag_sib(w, o):
-        ag_wait(w, o, (0, 8, 9, 10, 11, 12, 13, 14))
+        ag_wait(w, o, (0, 6, 9, 10, 13, 14, 15, 16))
 
     def ag_drain(w):
         for o in range(4):
-            for t in range(15):
-                m, d = ag_out[t]
-                b = block(w, o, m)
-                remote(b, b, ag_s.at[w, o, t], ag_r.at[w, o, t], d).wait_send()
+            for t in range(17):
+                ag_copy(w, o, t, ag_out[t][0]).wait_send()
 
     l_dout.wait()
     for o in range(4):
         buf_a[order[o], pl.ds(al(me * 48, 16), 48), :] = own_dout[
             :, pl.ds(al(order[o] * 768, 128), 768)
         ]
+        ag_sx(0, o)
         if o < 2:
-            ag_start(0, o)
+            ag_sy(0, o)
 
     l_tok.wait()
     x = own_tok[...].astype(F32)
@@ -185,6 +195,9 @@
         buf_b[o, pl.ds(al(me * 48, 16), 48), :] = (
             xhat[:, pl.ds(o * 768, 768)] * gain[:, pl.ds(o * 768, 768)]
         ).astype(BF16)
+
+    for o in range(4):
+        ag_sx(1, o)
 
     def att_fwd(b):
         rows = pl.ds(b * 256, 256)
@@ -211,26 +224,27 @@
     l_qkv.wait()
     att_fwd(0)
     ag_x(0, 0)
-    ag_start(0, 2)
     att_fwd(1)
+    ag_y(0, 0)
+    ag_sy(0, 2)
     ag_x(0, 1)
-    ag_start(0, 3)
     att_fwd(2)
-    ag_y(0, 0)
+    ag_yx(0, 0)
+    ag_y(0, 1)
+    ag_sy(0, 3)
     ag_x(0, 2)
     l_pre.wait()
     gelu(0)
     gelu(1)
-    ag_yx(0, 0)
+    ag_far(0, 0)
+    ag_yx(0, 1)
     ag_x(0, 3)
     gelu(2)
     gelu(3)
-    ag_y(0, 1)
-    ag_yx(0, 1)
+    ag_y(0, 2)
     gelu(4)
     gelu(5)
     ag_sib(0, 0)
-    ag_y(0, 2)
 
     class Ring:
         def __init__(self, src, rbuf, ssem, rsem, add):
@@ -274,42 +288,42 @@
             for cp in self.sent:
                 cp.wait_send()
 
-    def add_o(dst, src):
-        def step(i):
-            rows = pl.ds(al(i * 64, 64), 64)
-            for h in range(2):
-                dst[h, rows, :] = (
-                    dst[h, rows, :].astype(F32) + src[h, rows, :].astype(F32)
-                ).astype(BF16)
-
-        loop(HO // 64, step)
-
-    def add_i(dst, src):
-        def step(i):
-            rows = pl.ds(al(i * 16, 16), 16)
-            for h in range(2):
-                dst[h, rows, :] = (
-                    dst[h, rows, :].astype(F32) + src[h, rows, :].astype(F32)
-                ).astype(BF16)
-
-        loop(HI // 16, step)
-
-    def src_o(s):
-        return lambda zz, half: cout.at[
-            pl.ds(zz * 2, 2), pl.ds(s * 2 * HO + half * HO, HO), :
-        ]
-
-    def src_i(s):
-        return lambda zz, half: cin.at[
-            pl.ds(zz * 2, 2), pl.ds(s * 2 * HI + half * HI, HI), :
-        ]
-
-    ro = [Ring(src_o(s), rzo.at[s], zo_s.at[s], zo_r.at[s], add_o) for s in range(NSO)]
-    ri = [Ring(src_i(s), rzi.at[s], zi_s.at[s], zi_r.at[s], add_i) for s in range(NSI)]
+    def adder(lead, height, tile):
+        def add(dst, src):
+            def step(i):
+                rows = pl.ds(al(i * tile, tile), tile)
+                for at in lead:
+                    dst[at + (rows, slice(None))] = (
+                        dst[at + (rows, slice(None))].astype(F32)
+                        + src[at + (rows, slice(None))].astype(F32)
+                    ).astype(BF16)
+
+            loop(height // tile, step)
+
+        return add
+
+    def z_first(part, base, height):
+        return lambda zz, half: part.at[pl.ds(zz * 2, 2), pl.ds(base + half * height, height), :]
+
+    def x_first(part, base, height):
+        return lambda zz, half: part.at[zz * 2 + xh, pl.ds(base + half * height, height), :]
+
+    both = ((0,), (1,))
+    ro = [
+        Ring(z_first(cout, s * 2 * HO, HO), rzo.at[s], zo_s.at[s], zo_r.at[s], adder(both, HO, 64))
+        for s in range(NSO)
+    ]
+    ri = [
+        Ring(z_first(cin, s * 2 * HI, HI), rzi.at[s], zi_s.at[s], zi_r.at[s], adder(both, HI, 16))
+        for s in range(NSI)
+    ]
+    base_o, base_i = 1024 - XO, 384 - XI
+    fo = Ring(x_first(cout, base_o, XO // 2), rfo, fo_s, fo_r, adder(((),), XO // 2, 64))
+    fi = Ring(x_first(cin, base_i, XI // 2), rfi, fi_s, fi_r, adder(((),), XI // 2, 16))
 
     class Cross:
-        def __init__(self, ring, part, rx, out, ssem, rsem, base, height, tile):
-            self.ring, self.part, self.rx, self.out = ring, part, rx, out
+        def __init__(self, ring, part, rx, ssem, rsem, base, height, tile):
+            self.ring, self.part, self.rx = ring, part, rx
             self.ssem, self.rsem = ssem, rsem
             self.base, self.height, self.tile = base, height, tile
             self.sent = []
@@ -360,14 +374,66 @@
             for cp in self.sent:
                 cp.wait_send()
 
+    class First:
+        def __init__(self, ring, part, x1, rx, ssem, rsem, base, height, tile):
+            self.ring, self.part, self.x1, self.rx = ring, part, x1, rx
+            self.ssem, self.rsem = ssem, rsem
+            self.base, self.height, self.tile = base, height, tile
+
+        def copy(self, o):
+            return remote(
+                self.part.at[order[o] * 2 + xo, pl.ds(self.base, self.height), :],
+                self.x1.at[o], self.ssem.at[o], self.rsem.at[o], d_xo,
+            )
+
+        def send(self, o):
+            self.copy(o).start()
+
+        def take(self, o):
+            self.copy(o).wait_recv()
+
+            def step(i):
+                rows = pl.ds(al(i * self.tile, self.tile), self.tile)
+                prow = pl.ds(al(self.base + i * self.tile, self.tile), self.tile)
+                mine = order[o] * 2 + xh
+                self.part[mine, prow, :] = (
+                    self.part[mine, prow, :].astype(F32) + self.x1[o, rows, :].astype(F32)
+                ).astype(BF16)
+
+            loop(self.height // self.tile, step)
+            if o < 3:
+                (self.ring.far, self.ring.near_p, self.ring.near_m)[o]()
+
+        def finish(self):
+            self.ring.arrived()
+            r = self.ring.rbuf
+            half_rows = self.height // 2
+            for half, (a, b) in enumerate(((2, 5), (3, 4))):
+                off = self.base + half * half_rows
+
+                def step(i, a=a, b=b, off=off):
+                    rows = pl.ds(al(i * self.tile, self.tile), self.tile)
+                    prow = pl.ds(al(off + i * self.tile, self.tile), self.tile)
+                    self.rx[prow, :] = (
+                        r[a, rows, :].astype(F32)
+                        + r[b, rows, :].astype(F32)
+                        + self.part[z * 2 + xh, prow, :].astype(F32)
+                    ).astype(BF16)
+
+                loop(half_rows // self.tile, step)
+
+        def drain(self):
+            for o in range(4):
+                self.copy(o).wait_send()
+
     co = [
-        Cross(ro[s], cout, rxo, gwout, xo_s.at[s], xo_r.at[s], s * 2 * HO, HO, 64)
-        for s in range(NSO)
+        Cross(ro[s], cout, rxo, xo_s.at[s], xo_r.at[s], s * 2 * HO, HO, 64) for s in range(NSO)
     ]
     ci = [
-        Cross(ri[s], cin, rxi, gwin, xi_s.at[s], xi_r.at[s], s * 2 * HI, HI, 16)
-        for s in range(NSI)
+        Cross(ri[s], cin, rxi, xi_s.at[s], xi_r.at[s], s * 2 * HI, HI, 16) for s in range(NSI)
     ]
+    xfo = First(fo, cout, x1o, rxo, x1o_s, x1o_r, base_o, XO, 64)
+    xfi = First(fi, cin, x1i, rxi, x1i_s, x1i_r, base_i, XI, 16)
 
     def out_chunk(o):
         j = order[o]
@@ -383,25 +449,37 @@
     out_chunk(0)
     for r in ro:
         r.far()
+    xfo.send(0)
+    ag_far(0, 1)
     ag_yx(0, 2)
+    ag_y(0, 3)
+    ag_sy(1, 0)
     ag_sib(0, 1)
-    ag_y(0, 3)
     out_chunk(1)
     for r in ro:
         r.near_p()
+    xfo.send(1)
+    ag_far(0, 2)
     ag_yx(0, 3)
+    ag_x(1, 0)
+    ag_sy(1, 1)
     ag_sib(0, 2)
     out_chunk(2)
     for r in ro:
         r.near_m()
-    ag_start(1, 0)
-    ag_start(1, 1)
+    xfo.send(2)
+    ag_far(0, 3)
+    ag_x(1, 1)
+    ag_y(1, 0)
+    ag_sy(1, 2)
     ag_sib(0, 3)
     out_chunk(3)
-    ag_x(1, 0)
-    ag_x(1, 1)
-    ag_start(1, 2)
-    ag_start(1, 3)
+    xfo.send(3)
+    ag_yx(1, 0)
+    ag_y(1, 1)
+    ag_x(1, 2)
+    ag_sy(1, 3)
+    ag_x(1, 3)
 
     def joined_grad(nb):
         for l in wo_loads[nb]:
@@ -428,21 +506,20 @@
     joined_grad(0)
     for l in wo_loads[3]:
         l.start()
+    ag_far(1, 0)
+    ag_yx(1, 1)
     ro[0].relay_p()
     ro[0].relay_m()
-    ag_x(1, 2)
-    ag_x(1, 3)
     joined_grad(1)
-    ag_y(1, 0)
-    ag_y(1, 1)
+    ag_y(1, 2)
+    xfo.take(0)
     joined_grad(2)
-    ag_yx(1, 0)
-    ag_yx(1, 1)
-    joined_grad(3)
-    ag_y(1, 2)
-    ag_y(1, 3)
+    ag_far(1, 1)
+    ag_yx(1, 2)
     ro[1].relay_p()
     ro[1].relay_m()
+    joined_grad(3)
+    ag_y(1, 3)
 
     def win_load(j):
         return load(
@@ -470,10 +547,12 @@
             gproj[rows, pl.ds(256 + h * 128, 128)] = tn(ds, q).astype(BF16)
 
     att_bwd(0)
-    ag_yx(1, 2)
+    ag_far(1, 2)
     ag_yx(1, 3)
     att_bwd(1)
+    xfo.take(1)
     att_bwd(2)
+    ag_far(1, 3)
 
     ag_drain(0)
 
@@ -502,18 +581,24 @@
     in_chunk(0)
     for r in ri:
         r.far()
+    xfi.send(0)
     transposed(1)
     in_chunk(1)
     for r in ri:
         r.near_p()
+    xfi.send(1)
+    xfo.take(2)
     transposed(2)
     in_chunk(2)
     for r in ri:
         r.near_m()
+    xfi.send(2)
     transposed(3)
     in_chunk(3)
-    co[0].send()
-    co[1].send()
+    xfi.send(3)
+    xfo.take(3)
+    fo.relay_p()
+    fo.relay_m()
     ag_drain(1)
 
     def sib_copy(j):
@@ -598,19 +683,24 @@
     ri[1].relay_m()
     normed_grad(3)
     sib_sum(2)
+    co[0].send()
+    co[1].send()
+    sib_sum(3)
+    xfi.take(0)
+    ri[2].relay_p()
+    ri[2].relay_m()
+    y_sum(0)
+    y_sum(1)
+    xfi.take(1)
+    xfo.finish()
+    y_sum(2)
+    y_sum(3)
+    xfi.take(2)
     co[0].finish()
     co[1].finish()
     st_o = load(rxo, gwout, 0)
     st_o.start()
-    sib_sum(3)
-    y_sum(0)
-    ri[2].relay_p()
-    ri[2].relay_m()
-    y_sum(1)
-    y_sum(2)
-    y_sum(3)
-    ri[3].relay_p()
-    ri[3].relay_m()
+    xfi.take(3)
     for j in range(4):
         x_sum(j)
     xh_v = xhat[...]
@@ -622,13 +712,17 @@
     ).astype(BF16)
     st_g = load(own_tok, ig, 1)
     st_g.start()
-    for s in range(NSI):
-        ci[s].send()
+    ci[0].send()
+    fi.relay_p()
+    fi.relay_m()
+    ci[1].send()
+    ci[2].send()
     for s in range(NSI):
         ci[s].finish()
+    xfi.finish()
     st_i = load(rxi, gwin, 2)
     st_i.start()
-    for r in ro + ri + co + ci:
+    for r in ro + ri + [fo, fi] + co + ci + [xfo, xfi]:
         r.drain()
     for j in range(4):
         sib_copy(j).wait_send()
@@ -662,13 +756,17 @@
             v((768, 1536), BF16), v((1536, 1536), BF16), v((8, 1024, 384), BF16),
             v((8, 384, 1536), BF16),
             v((NSO, 6, 2, HO, 384), BF16), v((NSI, 6, 2, HI, 1536), BF16),
+            v((6, XO // 2, 384), BF16), v((6, XI // 2, 1536), BF16),
+            v((4, XO, 384), BF16), v((4, XI, 1536), BF16),
             v((1024, 384), BF16), v((384, 1536), BF16), v((4, 384, 768), BF16),
             v((3, 4, 96, 768), BF16), v((4, 48, 768), BF16), v((4, 48, 768), BF16),
             v((48, 3072), F32), v((48, 3072), F32), v((48, 3072), BF16),
             v((48, 3072), BF16), v((48, 128), F32),
-            sem((16,)), sem((2, 4, 15)), sem((2, 4, 15)),
+            sem((16,)), sem((2, 4, 17)), sem((2, 4, 17)),
             sem((NSO, 6)), sem((NSO, 6)), sem((NSI, 6)), sem((NSI, 6)),
+            sem((6,)), sem((6,)), sem((6,)), sem((6,)),
             sem((NSO, 2)), sem((NSO, 2)), sem((NSI, 2)), sem((NSI, 2)),
+            sem((4,)), sem((4,)), sem((4,)), sem((4,)),
             sem((4,)), sem((4,)), sem((3, 4)), sem((3, 4)), sem((4,)), sem((4,)),
         ],
         compiler_params=pltpu.CompilerParams(

time: 175 us -> 144 us (0.82)
  Pallas kernels: 169 us -> 139 us
    pallas_call x1, Pallas kernels: 169 us -> 139 us  [body(): pl.pallas_call(kernel, name='block_backward', out_shape=(jax.ShapeDtypeSt...]
where the time goes in v2:
time: 144 us
  Pallas kernels  139 us (97%)
  other arithmetic  4.28 us (3%)
    pallas_call x1, Pallas kernels, body(): pl.pallas_call(kernel, name='block_backward', out_shape=(jax.ShapeDtypeSt...  139 us
    convert_element_type x2, other arithmetic, body(): return (ig, gwin.astype(F32), gwout.astype(F32))  4.28 us

profile of v2, /device:TPU:0, one launch (start us, length us, event | category | flops | bytes accessed | tf_op | source)
XLA Modules:
  0.0 144.2 jit_solution(14635190379617707587)
XLA Ops:
  0.6 138.5 %block_backward.1 = (bf16[48,3072]{1,0:T(8,128)(2,1)}, bf16[384,1536]{1,0:T(8,128)(2,1)}, bf16[1024,384]{1,0:T(8,128)(2,1)}) custom-call(bf16[48,3072]{1,0:T(8,128)(2,1)} %tok.1, f32[1,3072]{1,0:T(1,128)} %bitcast.1, bf16[3072,1536]{1,0:T(8,128)(2,1)} %win.1, bf16[1024,3072]{1,0:T(8,128)(2,1)} %wout.1, bf16[768,768]{1,0:T(8,128)(2,1)} %qkv_hbm.1, ...), custom_call_target="tpu_custom_call" | custom-call | tf_op jit(solution)/shard_map/block_backward/pallas_call | solution.py:742
  139.2 0.0 copy-start
  139.2 3.0 %convert_element_type.6 = f32[384,1536]{1,0:T(8,128)} convert(bf16[384,1536]{1,0:T(8,128)(2,1)} %get-tuple-element.7) | non-fusion elementwise | flops 589824 | bytes 3538944 | tf_op jit(solution)/shard_map/convert_element_type | solution.py:779
  142.2 0.0 copy-start.1
  142.2 0.0 copy-done
  142.2 1.2 convert_element_type.7
  143.5 0.0 copy-done.1
  143.5 0.7 copy.11
Async XLA Ops:
  139.2 3.1 %copy-start = (bf16[1024,384]{1,0:T(8,128)(2,1)S(1)}, bf16[1024,384]{1,0:T(8,128)(2,1)}, u32[]{:S(2)}) copy-start(bf16[1024,384]{1,0:T(8,128)(2,1)} %get-tuple-element.8) | copy-start | bytes 2359300
  142.2 1.3 copy-start.1

commit v3 on v2

--- a/solution.py
+++ b/solution.py
@@ -44,9 +44,10 @@
     tok, gain, win, wout, qkv_hbm, pre_hbm, dout,
     ig, gwin, gwout,
     buf_a, buf_b, qkv, pre, slope, pf, heads, joined_t, gh, gproj, wslot, cout, cin,
-    rzo, rzi, rfo, rfi, x1o, x1i, rxo, rxi, rs_sib, rs_y, rs_x, ss_x, xhat, gn, own_tok, own_dout, rstd_ref,
+    rzo, rzi, rfo, rfi, x1o, x1i, rxo, rxi, rs_sib, rs_y, rs_x, ss_x, xhat, gn,
+    own_tok, own_dout, rstd_ref,
     lsem, ag_s, ag_r, zo_s, zo_r, zi_s, zi_r, fo_s, fo_r, fi_s, fi_r, xo_s, xo_r, xi_s, xi_r,
-    x1o_s, x1o_r, x1i_s, x1i_r, ms_s, ms_r, my_s, my_r, mx_s, mx_r,
+    x1o_s, x1o_r, x1i_s, x1i_r, m_s, ms_r, my_r, mx_r,
 ):
     dp = lax.axis_index("dp")
     mp = lax.axis_index("mp")
@@ -75,8 +76,10 @@
     def load(src, dst, i):
         return pltpu.make_async_copy(src, dst, lsem.at[i])
 
-    l_dout = load(dout, own_dout, 0)
-    l_tok = load(tok, own_tok, 1)
+    own = 2 * y + xl
+    order = (z2, zp, zm, z)
+    l_dout = load(dout, own_dout, 12)
+    l_tok = load(tok, own_tok, 0)
     l_qkv = load(qkv_hbm, qkv, 2)
     l_pre = load(pre_hbm, pre, 3)
     for l in (l_dout, l_tok, l_qkv, l_pre):
@@ -108,78 +111,53 @@
             src_ref=src, dst_ref=dst, send_sem=s, recv_sem=r, device_id=d, device_id_type=MESH
         )
 
-    order = (z2, zp, zm, z)
-    me = m_of(y, xl, c)
-    mx = m_of(y, xn, c)
-    b_ym, b_yp, b_y2 = m_of(ym, xl, c), m_of(yp, xl, c), m_of(y2, xl, c)
-    b_xym, b_xyp, b_xy2 = m_of(ym, xn, c), m_of(yp, xn, c), m_of(y2, xn, c)
-    ag_out = (
-        (me, 0, d_sib), (me, 0, d_xn), (me, 0, d_yp), (me, 0, d_ym),
-        (mx, 0, d_yp), (mx, 0, d_ym), (mx, 0, d_sib),
-        (b_ym, 1, d_yp), (b_yp, 2, d_ym), (b_ym, 0, d_sib), (b_yp, 0, d_sib),
-        (b_xym, 1, d_yp), (b_xyp, 2, d_ym), (b_xym, 0, d_sib), (b_xyp, 0, d_sib),
-        (b_y2, 0, d_sib), (b_xy2, 0, d_sib),
-    )
-    ag_in = (
-        m_of(y, xl, cn), mx, b_ym, b_yp, b_xym, b_xyp, m_of(y, xn, cn),
-        b_y2, b_y2, m_of(ym, xl, cn), m_of(yp, xl, cn),
-        b_xy2, b_xy2, m_of(ym, xn, cn), m_of(yp, xn, cn), m_of(y2, xl, cn), m_of(y2, xn, cn),
-    )
     bufs = (buf_a, buf_b)
-
-    def block(w, o, m, part):
-        cols = (slice(None), pl.ds(0, 384), pl.ds(384, 384))[part]
-        return bufs[w].at[order[o], pl.ds(al(m * 48, 16), 48), cols]
-
-    def ag_copy(w, o, t, m):
-        b = block(w, o, m, ag_out[t][1])
-        return remote(b, b, ag_s.at[w, o, t], ag_r.at[w, o, t], ag_out[t][2])
-
-    def ag_send(w, o, ts):
-        for t in ts:
-            ag_copy(w, o, t, ag_out[t][0]).start()
-
-    def ag_wait(w, o, ts):
-        for t in ts:
-            ag_copy(w, o, t, ag_in[t]).wait_recv()
+    pair, pair_p, pair_m, pair_2 = (pl.ds(2 * v, 2) for v in (y, yp, ym, y2))
+    whole, left, right = slice(None), pl.ds(0, 384), pl.ds(384, 384)
+
+    def ag_copy(w, o, kind, at, core, cols, d):
+        b = bufs[w].at[order[o], at, core, :, cols]
+        sent = ag_s.at[w, 0 if kind == 0 else 1]
+        return remote(b, b, sent, ag_r.at[w, o, kind], d)
+
+    def ag_wait(w, o, kind, at, core):
+        ag_copy(w, o, kind, at, core, whole, d_sib).wait_recv()
 
     def ag_sx(w, o):
-        ag_send(w, o, (1,))
+        ag_copy(w, o, 0, own, c, whole, d_xn).start()
 
     def ag_sy(w, o):
-        ag_send(w, o, (2, 3, 0))
+        ag_copy(w, o, 1, own, c, whole, d_yp).start()
+        ag_copy(w, o, 1, own, c, whole, d_ym).start()
 
     def ag_x(w, o):
-        ag_wait(w, o, (1,))
-        ag_send(w, o, (4, 5, 6))
+        ag_wait(w, o, 0, 2 * y + xn, c)
+        at = 2 * y + xn if w == 0 and o < 2 else pair
+        ag_copy(w, o, 1, at, c, whole, d_yp).start()
+        ag_copy(w, o, 1, at, c, whole, d_ym).start()
+        ag_copy(w, o, 3, pair, c, whole, d_sib).start()
 
     def ag_y(w, o):
-        ag_wait(w, o, (2, 3))
-        ag_send(w, o, (7, 8, 9, 10))
-
-    def ag_yx(w, o):
-        ag_wait(w, o, (4, 5))
-        ag_send(w, o, (11, 12, 13, 14))
+        ag_wait(w, o, 1, pl.ds(0, 4), c)
+        ag_copy(w, o, 2, pair_m, c, left, d_yp).start()
+        ag_copy(w, o, 2, pair_p, c, right, d_ym).start()
+        ag_copy(w, o, 3, pair_m, c, whole, d_sib).start()
+        ag_copy(w, o, 3, pair_p, c, whole, d_sib).start()
 
     def ag_far(w, o):
-        ag_wait(w, o, (7, 8))
-        ag_send(w, o, (15,))
-        ag_wait(w, o, (11, 12))
-        ag_send(w, o, (16,))
+        ag_wait(w, o, 2, pair_2, c)
+        ag_copy(w, o, 3, pair_2, c, whole, d_sib).start()
 
     def ag_sib(w, o):
-        ag_wait(w, o, (0, 6, 9, 10, 13, 14, 15, 16))
+        ag_wait(w, o, 3, whole, cn)
 
     def ag_drain(w):
-        for o in range(4):
-            for t in range(17):
-                ag_copy(w, o, t, ag_out[t][0]).wait_send()
+        for i, b in enumerate((bufs[w].at[:, own, c], bufs[w].at[:, pl.ds(0, 7)])):
+            remote(b, b, ag_s.at[w, i], ag_r.at[w, 0, 0], d_sib).wait_send()
 
     l_dout.wait()
     for o in range(4):
-        buf_a[order[o], pl.ds(al(me * 48, 16), 48), :] = own_dout[
-            :, pl.ds(al(order[o] * 768, 128), 768)
-        ]
+        buf_a[order[o], own, c] = own_dout[:, pl.ds(al(order[o] * 768, 128), 768)]
         ag_sx(0, o)
         if o < 2:
             ag_sy(0, o)
@@ -192,7 +170,7 @@
     xhat[...] = (x - center) * rstd
     rstd_ref[...] = jnp.broadcast_to(rstd, rstd_ref.shape)
     for o in range(4):
-        buf_b[o, pl.ds(al(me * 48, 16), 48), :] = (
+        buf_b[o, own, c] = (
             xhat[:, pl.ds(o * 768, 768)] * gain[:, pl.ds(o * 768, 768)]
         ).astype(BF16)
 
@@ -221,29 +199,24 @@
         dens = jnp.exp(-0.5 * v * v) * 0.3989422804014327
         slope[rows, :] = cumul + v * dens
 
-    l_qkv.wait()
-    att_fwd(0)
-    ag_x(0, 0)
-    att_fwd(1)
-    ag_y(0, 0)
-    ag_sy(0, 2)
-    ag_x(0, 1)
-    att_fwd(2)
-    ag_yx(0, 0)
-    ag_y(0, 1)
-    ag_sy(0, 3)
-    ag_x(0, 2)
     l_pre.wait()
     gelu(0)
+    ag_x(0, 0)
+    l_qkv.wait()
     gelu(1)
-    ag_far(0, 0)
-    ag_yx(0, 1)
-    ag_x(0, 3)
+    ag_x(0, 1)
+    att_fwd(0)
+    att_fwd(1)
+    att_fwd(2)
     gelu(2)
+    ag_y(0, 0)
+    ag_x(0, 2)
     gelu(3)
-    ag_y(0, 2)
     gelu(4)
     gelu(5)
+    ag_y(0, 1)
+    ag_x(0, 3)
+    ag_far(0, 0)
     ag_sib(0, 0)
 
     class Ring:
@@ -440,7 +413,7 @@
 
         def step(r):
             rows = pl.ds(al(r * 256, 256), 256)
-            t = nn(joined_t[rows, :], buf_a[j]).astype(BF16)
+            t = nn(joined_t[rows, :], buf_a[j].reshape(768, 768)).astype(BF16)
             cout[j * 2, rows, :] = t[:, :384]
             cout[j * 2 + 1, rows, :] = t[:, 384:]
 
@@ -451,35 +424,34 @@
         r.far()
     xfo.send(0)
     ag_far(0, 1)
-    ag_yx(0, 2)
-    ag_y(0, 3)
-    ag_sy(1, 0)
+    ag_y(0, 2)
     ag_sib(0, 1)
     out_chunk(1)
     for r in ro:
         r.near_p()
     xfo.send(1)
     ag_far(0, 2)
-    ag_yx(0, 3)
+    ag_y(0, 3)
     ag_x(1, 0)
-    ag_sy(1, 1)
+    ag_x(1, 1)
     ag_sib(0, 2)
     out_chunk(2)
     for r in ro:
         r.near_m()
     xfo.send(2)
     ag_far(0, 3)
-    ag_x(1, 1)
+    ro[0].relay_p()
+    ro[0].relay_m()
     ag_y(1, 0)
-    ag_sy(1, 2)
+    ag_x(1, 2)
     ag_sib(0, 3)
     out_chunk(3)
     xfo.send(3)
-    ag_yx(1, 0)
     ag_y(1, 1)
-    ag_x(1, 2)
-    ag_sy(1, 3)
     ag_x(1, 3)
+    ag_far(1, 0)
+    ro[1].relay_p()
+    ro[1].relay_m()
 
     def joined_grad(nb):
         for l in wo_loads[nb]:
@@ -491,7 +463,7 @@
             acc = jnp.zeros((384, 256), F32)
             for j in range(4):
                 w = wslot[pl.ds(row + (j // 2) * 256, 256), pl.ds((j % 2) * 768, 768)]
-                acc = acc + nt(buf_a[j, rows, :], w)
+                acc = acc + nt(buf_a[j, pl.ds(r * 4, 4)].reshape(384, 768), w)
             g = acc.astype(BF16)
             if nb == 0:
                 gh[rows, :] = g
@@ -506,24 +478,18 @@
     joined_grad(0)
     for l in wo_loads[3]:
         l.start()
-    ag_far(1, 0)
-    ag_yx(1, 1)
-    ro[0].relay_p()
-    ro[0].relay_m()
     joined_grad(1)
+    ag_far(1, 1)
     ag_y(1, 2)
     xfo.take(0)
     joined_grad(2)
-    ag_far(1, 1)
-    ag_yx(1, 2)
-    ro[1].relay_p()
-    ro[1].relay_m()
     joined_grad(3)
+    ag_far(1, 2)
     ag_y(1, 3)
 
     def win_load(j):
         return load(
-            win.at[pl.ds(j * 768, 768), :], wslot.at[pl.ds((j % 2) * 768, 768)], 12 + j
+            win.at[pl.ds(j * 768, 768), :], wslot.at[pl.ds((j % 2) * 768, 768)], 4 + j
         )
 
     win_load(0).start()
@@ -547,12 +513,9 @@
             gproj[rows, pl.ds(256 + h * 128, 128)] = tn(ds, q).astype(BF16)
 
     att_bwd(0)
-    ag_far(1, 2)
-    ag_yx(1, 3)
     att_bwd(1)
+    att_bwd(2)
     xfo.take(1)
-    att_bwd(2)
-    ag_far(1, 3)
 
     ag_drain(0)
 
@@ -561,19 +524,20 @@
         j = order[o]
 
         def step(i):
-            rows = pl.ds(al(i * 128, 128), 128)
-            buf_a[j, :, rows] = jnp.transpose(buf_b[j, rows, :])
-
-        loop(6, step)
+            block = buf_b[j, pl.ds(i * 4, 4)].reshape(384, 768)
+            rows = pl.ds(al(i * 384, 128), 384)
+            buf_a[j, :, :, :, rows] = jnp.transpose(block).reshape(8, 2, 48, 384)
+
+        loop(2, step)
 
     def in_chunk(o):
         j = order[o]
 
         def step(i):
             h, n = i // 2, i % 2
-            rows = pl.ds(al(h * 384, 128), 384)
             cols = pl.ds(al(n * 768, 128), 768)
-            cin[j * 2 + h, :, cols] = nn(buf_a[j, rows, :], gproj[:, cols]).astype(BF16)
+            left_side = buf_a[j, pl.ds(h * 4, 4)].reshape(384, 768)
+            cin[j * 2 + h, :, cols] = nn(left_side, gproj[:, cols]).astype(BF16)
 
         loop(4, step)
 
@@ -582,30 +546,24 @@
     for r in ri:
         r.far()
     xfi.send(0)
+    ag_far(1, 3)
     transposed(1)
     in_chunk(1)
-    for r in ri:
-        r.near_p()
+    ri[0].near_p()
     xfi.send(1)
     xfo.take(2)
     transposed(2)
     in_chunk(2)
-    for r in ri:
-        r.near_m()
+    ri[0].near_m()
     xfi.send(2)
     transposed(3)
     in_chunk(3)
     xfi.send(3)
     xfo.take(3)
-    fo.relay_p()
-    fo.relay_m()
     ag_drain(1)
 
     def sib_copy(j):
-        return remote(
-            buf_b.at[j, pl.ds(al(cn * 384, 128), 384), :], rs_sib.at[j],
-            ms_s.at[j], ms_r.at[j], d_sib,
-        )
+        return remote(buf_b.at[j, :, cn], rs_sib.at[j], m_s.at[0], ms_r.at[j], d_sib)
 
     def normed_grad(j):
         win_load(j).wait()
@@ -617,50 +575,35 @@
             w = wslot[pl.ds(al(base + n * 256, 256), 256), :]
             t = nt(gproj[rows, :], w).astype(BF16)
             cols = pl.ds(al(n * 256, 128), 256)
-            for b in range(8):
-                buf_b[j, pl.ds(al((b % 2) * 384 + (h * 4 + b // 2) * 48, 16), 48), cols] = t[
-                    b * 48 : b * 48 + 48
-                ]
+            buf_b[j, pl.ds(h * 4, 4), :, :, cols] = t.reshape(4, 2, 48, 256)
 
         loop(6, step)
         sib_copy(j).start()
         if j < 2:
             win_load(j + 2).start()
 
-    y_rows = {0: yp, 1: ym, 2: y2}
-    y_dev = (d_yp, d_ym, d_y2)
-
-    def y_copy(j, i):
-        return remote(
-            buf_b.at[j, pl.ds(al(c * 384 + y_rows[i] * 96, 16), 96), :], rs_y.at[i, j],
-            my_s.at[i, j], my_r.at[i, j], y_dev[i],
-        )
+    y_out = ((pair_p, d_yp), (pair_m, d_ym), (pair_2, d_y2))
 
     def sib_sum(j):
         sib_copy(j).wait_recv()
 
         def step(i):
-            rows = pl.ds(al(c * 384 + i * 48, 16), 48)
-            buf_b[j, rows, :] = (
-                buf_b[j, rows, :].astype(F32)
-                + rs_sib[j, pl.ds(al(i * 48, 16), 48), :].astype(F32)
-            ).astype(BF16)
+            buf_b[j, i, c] = (buf_b[j, i, c].astype(F32) + rs_sib[j, i].astype(F32)).astype(BF16)
 
         loop(8, step)
-        for i in range(3):
-            y_copy(j, i).start()
+        for i, (at, d) in enumerate(y_out):
+            remote(buf_b.at[j, at, c], rs_y.at[j, i], m_s.at[1], my_r.at[j], d).start()
 
     def x_copy(j):
-        return remote(ss_x.at[j], rs_x.at[j], mx_s.at[j], mx_r.at[j], d_xn)
+        return remote(ss_x.at[j], rs_x.at[j], m_s.at[2], mx_r.at[j], d_xn)
 
     def y_sum(j):
-        for i in range(3):
-            y_copy(j, i).wait_recv()
+        remote(rs_y.at[j], rs_y.at[j], m_s.at[1], my_r.at[j], d_yp).wait_recv()
 
         def total(side):
-            acc = buf_b[j, pl.ds(al(c * 384 + y * 96 + side * 48, 16), 48), :].astype(F32)
+            acc = buf_b[j, 2 * y + side, c].astype(F32)
             for i in range(3):
-                acc = acc + rs_y[i, j, pl.ds(al(side * 48, 16), 48), :].astype(F32)
+                acc = acc + rs_y[j, i, side].astype(F32)
             return acc
 
         ss_x[j] = total(xn).astype(BF16)
@@ -675,32 +618,36 @@
     normed_grad(0)
     ri[0].relay_p()
     ri[0].relay_m()
+    ri[1].near_p()
+    ri[1].near_m()
     normed_grad(1)
     sib_sum(0)
+    co[0].send()
+    co[1].send()
     normed_grad(2)
-    sib_sum(1)
     ri[1].relay_p()
     ri[1].relay_m()
+    ri[2].near_p()
+    ri[2].near_m()
+    sib_sum(1)
     normed_grad(3)
-    sib_sum(2)
-    co[0].send()
-    co[1].send()
-    sib_sum(3)
-    xfi.take(0)
     ri[2].relay_p()
     ri[2].relay_m()
+    fo.relay_p()
+    fo.relay_m()
+    sib_sum(2)
+    xfi.take(0)
+    sib_sum(3)
     y_sum(0)
+    xfi.take(1)
     y_sum(1)
-    xfi.take(1)
-    xfo.finish()
+    xfi.take(2)
     y_sum(2)
     y_sum(3)
-    xfi.take(2)
+    xfi.take(3)
     co[0].finish()
     co[1].finish()
-    st_o = load(rxo, gwout, 0)
-    st_o.start()
-    xfi.take(3)
+    ci[0].send()
     for j in range(4):
         x_sum(j)
     xh_v = xhat[...]
@@ -710,33 +657,38 @@
     own_tok[...] = (
         own_dout[...].astype(F32) + (sg - m1 - xh_v * m2) * rstd_ref[:, :1]
     ).astype(BF16)
-    st_g = load(own_tok, ig, 1)
+    st_g = load(own_tok, ig, 0)
     st_g.start()
-    ci[0].send()
+    ci[1].send()
+    ci[0].finish()
+    ci[1].finish()
+    ci[2].send()
+    xfo.finish()
+    st_o = load(rxo, gwout, 1)
+    st_o.start()
     fi.relay_p()
     fi.relay_m()
-    ci[1].send()
-    ci[2].send()
-    for s in range(NSI):
-        ci[s].finish()
+    st_i = [
+        load(rxi.at[pl.ds(a, n)], gwin.at[pl.ds(a, n)], 2 + i)
+        for i, (a, n) in enumerate(((0, 4 * HI), (4 * HI, 2 * HI), (base_i, XI)))
+    ]
+    st_i[0].start()
     xfi.finish()
-    st_i = load(rxi, gwin, 2)
-    st_i.start()
+    st_i[2].start()
+    ci[2].finish()
+    st_i[1].start()
     for r in ro + ri + [fo, fi] + co + ci + [xfo, xfi]:
         r.drain()
-    for j in range(4):
-        sib_copy(j).wait_send()
-        x_copy(j).wait_send()
-        for i in range(3):
-            y_copy(j, i).wait_send()
+    for b, i in ((rs_sib, 0), (rs_y, 1), (rs_x, 2)):
+        remote(b, b, m_s.at[i], mx_r.at[0], d_sib).wait_send()
     st_o.wait()
     st_g.wait()
-    st_i.wait()
+    for st in st_i:
+        st.wait()
 
 
 def body(block_input_tokens, norm_gain_vector, w_in, w_out, saved_qkv, mlp_pre, output_gradient):
     hbm = pl.BlockSpec(memory_space=pl.ANY)
-    vmem = pl.BlockSpec(memory_space=pltpu.VMEM)
     sem = pltpu.SemaphoreType.DMA
     v = pltpu.VMEM
     ig, gwin, gwout = pl.pallas_call(
@@ -747,10 +699,10 @@
             jax.ShapeDtypeStruct((384, 1536), BF16),
             jax.ShapeDtypeStruct((1024, 384), BF16),
         ),
-        in_specs=[hbm, vmem, hbm, hbm, hbm, hbm, hbm],
+        in_specs=[hbm, pl.BlockSpec(memory_space=pltpu.VMEM), hbm, hbm, hbm, hbm, hbm],
         out_specs=(hbm, hbm, hbm),
         scratch_shapes=[
-            v((4, 768, 768), BF16), v((4, 768, 768), BF16), v((768, 768), BF16),
+            v((4, 8, 2, 48, 768), BF16), v((4, 8, 2, 48, 768), BF16), v((768, 768), BF16),
             v((768, 768), BF16), v((768, 768), F32), v((6, 256, 256), F32),
             v((768, 256), BF16), v((1024, 768), BF16), v((768, 256), BF16),
             v((768, 1536), BF16), v((1536, 1536), BF16), v((8, 1024, 384), BF16),
@@ -758,16 +710,15 @@
             v((NSO, 6, 2, HO, 384), BF16), v((NSI, 6, 2, HI, 1536), BF16),
             v((6, XO // 2, 384), BF16), v((6, XI // 2, 1536), BF16),
             v((4, XO, 384), BF16), v((4, XI, 1536), BF16),
-            v((1024, 384), BF16), v((384, 1536), BF16), v((4, 384, 768), BF16),
-            v((3, 4, 96, 768), BF16), v((4, 48, 768), BF16), v((4, 48, 768), BF16),
+            v((1024, 384), BF16), v((384, 1536), BF16), v((4, 8, 48, 768), BF16),
+            v((4, 3, 2, 48, 768), BF16), v((4, 48, 768), BF16), v((4, 48, 768), BF16),
             v((48, 3072), F32), v((48, 3072), F32), v((48, 3072), BF16),
             v((48, 3072), BF16), v((48, 128), F32),
-            sem((16,)), sem((2, 4, 17)), sem((2, 4, 17)),
+            sem((16,)), sem((2, 2)), sem((2, 4, 4)),
             sem((NSO, 6)), sem((NSO, 6)), sem((NSI, 6)), sem((NSI, 6)),
             sem((6,)), sem((6,)), sem((6,)), sem((6,)),
             sem((NSO, 2)), sem((NSO, 2)), sem((NSI, 2)), sem((NSI, 2)),
-            sem((4,)), sem((4,)), sem((4,)), sem((4,)),
-            sem((4,)), sem((4,)), sem((3, 4)), sem((3, 4)), sem((4,)), sem((4,)),
+            sem((4,)), sem((4,)), sem((4,)), sem((4,)), sem((3,)), sem((4,)), sem((4,)), sem((4,)),
         ],
         compiler_params=pltpu.CompilerParams(
             collective_id=0, has_side_effects=True, vmem_limit_bytes=63 << 20

time: 144 us -> 139 us (0.965); the launches traced: 144 us -> 137 us
  Pallas kernels: 139 us -> 132 us
    pallas_call x1, Pallas kernels: 139 us -> 132 us  [body(): pl.pallas_call(kernel, name='block_backward', out_shape=(jax.ShapeDtypeSt...]
where the time goes in v3:
time: 139 us; the launch traced here: 137 us
  Pallas kernels  132 us (95%)
  other arithmetic  4.28 us (3%)
    pallas_call x1, Pallas kernels, body(): pl.pallas_call(kernel, name='block_backward', out_shape=(jax.ShapeDtypeSt...  132 us
    convert_element_type x2, other arithmetic, body(): return (ig, gwin.astype(F32), gwout.astype(F32))  4.28 us

profile of v3, /device:TPU:0, one launch (start us, length us, event | category | flops | bytes accessed | tf_op | source)
XLA Modules:
  0.0 137.3 jit_solution(9416258618467488574)
XLA Ops:
  0.6 131.7 %block_backward.1 = (bf16[48,3072]{1,0:T(8,128)(2,1)}, bf16[384,1536]{1,0:T(8,128)(2,1)}, bf16[1024,384]{1,0:T(8,128)(2,1)}) custom-call(bf16[48,3072]{1,0:T(8,128)(2,1)} %tok.1, f32[1,3072]{1,0:T(1,128)} %bitcast.1, bf16[3072,1536]{1,0:T(8,128)(2,1)} %win.1, bf16[1024,3072]{1,0:T(8,128)(2,1)} %wout.1, bf16[768,768]{1,0:T(8,128)(2,1)} %qkv_hbm.1, ...), custom_call_target="tpu_custom_call" | custom-call | tf_op jit(solution)/shard_map/block_backward/pallas_call | solution.py:694
  132.3 0.0 copy-start
  132.3 3.0 %convert_element_type.6 = f32[384,1536]{1,0:T(8,128)} convert(bf16[384,1536]{1,0:T(8,128)(2,1)} %get-tuple-element.7) | non-fusion elementwise | flops 589824 | bytes 3538944 | tf_op jit(solution)/shard_map/convert_element_type | solution.py:730
  135.4 0.0 copy-start.1
  135.4 0.0 copy-done
  135.4 1.2 convert_element_type.7
  136.6 0.0 copy-done.1
  136.6 0.7 copy.11
Async XLA Ops:
  132.3 3.1 %copy-start = (bf16[1024,384]{1,0:T(8,128)(2,1)S(1)}, bf16[1024,384]{1,0:T(8,128)(2,1)}, u32[]{:S(2)}) copy-start(bf16[1024,384]{1,0:T(8,128)(2,1)} %get-tuple-element.8) | copy-start | bytes 2359300
  135.4 1.3 copy-start.1

commit v4 on v3

--- a/solution.py
+++ b/solution.py
@@ -12,8 +12,8 @@
 BF16 = jnp.bfloat16
 SCALE = HD ** (-0.5)
 MESH = pl.DeviceIdType.MESH
-NSO, HO, XO = 2, 128, 512
-NSI, HI, XI = 3, 48, 96
+NSO, HO, XO = 3, 128, 256
+BLOCKS = (3, 4, 5, 2, 0, 1)
 
 
 def nt(a, b):
@@ -33,7 +33,10 @@
         fn(i)
         return carry
 
-    lax.fori_loop(0, n, step, 0)
+    if n == 1:
+        fn(0)
+    else:
+        lax.fori_loop(0, n, step, 0)
 
 
 def al(v, m):
@@ -41,13 +44,13 @@
 
 
 def kernel(
-    tok, gain, win, wout, qkv_hbm, pre_hbm, dout,
+    tok, gain_hbm, win, wout, qkv_hbm, pre_hbm, dout,
     ig, gwin, gwout,
-    buf_a, buf_b, qkv, pre, slope, pf, heads, joined_t, gh, gproj, wslot, cout, cin,
-    rzo, rzi, rfo, rfi, x1o, x1i, rxo, rxi, rs_sib, rs_y, rs_x, ss_x, xhat, gn,
+    buf_a, buf_b, qkv, pre, slope, pf, heads, joined_t, gh, gproj, gp2, wslot, cout, cin,
+    rzo, rzi, rfo, x1o, rxo, rxi, nsend, rs_sib, rs_y, rs_x, ss_x, xhat, gn, gain,
     own_tok, own_dout, rstd_ref,
-    lsem, ag_s, ag_r, zo_s, zo_r, zi_s, zi_r, fo_s, fo_r, fi_s, fi_r, xo_s, xo_r, xi_s, xi_r,
-    x1o_s, x1o_r, x1i_s, x1i_r, m_s, ms_r, my_r, mx_r,
+    lsem, ag_s, ag_r, zo_s, zo_r, zi_s, zi_r, fo_s, fo_r, xo_s, xo_r,
+    x1o_s, x1o_r, gx_s, gx_r, nx_s, m_s, ms_r, my_r, mx_r,
 ):
     dp = lax.axis_index("dp")
     mp = lax.axis_index("mp")
@@ -80,9 +83,10 @@
     order = (z2, zp, zm, z)
     l_dout = load(dout, own_dout, 12)
     l_tok = load(tok, own_tok, 0)
+    l_gain = load(gain_hbm, gain, 1)
     l_qkv = load(qkv_hbm, qkv, 2)
     l_pre = load(pre_hbm, pre, 3)
-    for l in (l_dout, l_tok, l_qkv, l_pre):
+    for l in (l_dout, l_tok, l_gain, l_qkv, l_pre):
         l.start()
 
     def wout_loads(nb, row):
@@ -95,9 +99,9 @@
             for h in range(2)
         ]
 
-    wo_rows = (0, 512, 1024, 0)
+    wo_rows = (0, 0, 512, 1024)
     wo_loads = [wout_loads(nb, wo_rows[nb]) for nb in range(4)]
-    for nb in range(3):
+    for nb in range(1, 4):
         for l in wo_loads[nb]:
             l.start()
 
@@ -113,43 +117,42 @@
 
     bufs = (buf_a, buf_b)
     pair, pair_p, pair_m, pair_2 = (pl.ds(2 * v, 2) for v in (y, yp, ym, y2))
-    whole, left, right = slice(None), pl.ds(0, 384), pl.ds(384, 384)
-
-    def ag_copy(w, o, kind, at, core, cols, d):
+    full = tuple((o, slice(None)) for o in range(4))
+    chunks = (((0, pl.ds(0, 384)), (0, pl.ds(384, 384))) + full[1:], full)
+
+    def ag_copy(w, k, kind, at, core, d):
+        o, cols = chunks[w][k]
         b = bufs[w].at[order[o], at, core, :, cols]
         sent = ag_s.at[w, 0 if kind == 0 else 1]
-        return remote(b, b, sent, ag_r.at[w, o, kind], d)
-
-    def ag_wait(w, o, kind, at, core):
-        ag_copy(w, o, kind, at, core, whole, d_sib).wait_recv()
-
-    def ag_sx(w, o):
-        ag_copy(w, o, 0, own, c, whole, d_xn).start()
-
-    def ag_sy(w, o):
-        ag_copy(w, o, 1, own, c, whole, d_yp).start()
-        ag_copy(w, o, 1, own, c, whole, d_ym).start()
-
-    def ag_x(w, o):
-        ag_wait(w, o, 0, 2 * y + xn, c)
-        at = 2 * y + xn if w == 0 and o < 2 else pair
-        ag_copy(w, o, 1, at, c, whole, d_yp).start()
-        ag_copy(w, o, 1, at, c, whole, d_ym).start()
-        ag_copy(w, o, 3, pair, c, whole, d_sib).start()
-
-    def ag_y(w, o):
-        ag_wait(w, o, 1, pl.ds(0, 4), c)
-        ag_copy(w, o, 2, pair_m, c, left, d_yp).start()
-        ag_copy(w, o, 2, pair_p, c, right, d_ym).start()
-        ag_copy(w, o, 3, pair_m, c, whole, d_sib).start()
-        ag_copy(w, o, 3, pair_p, c, whole, d_sib).start()
-
-    def ag_far(w, o):
-        ag_wait(w, o, 2, pair_2, c)
-        ag_copy(w, o, 3, pair_2, c, whole, d_sib).start()
-
-    def ag_sib(w, o):
-        ag_wait(w, o, 3, whole, cn)
+        return remote(b, b, sent, ag_r.at[w, k, kind], d)
+
+    def ag_sx(w, k):
+        ag_copy(w, k, 0, own, c, d_xn).start()
+
+    def ag_sy(w, k):
+        ag_copy(w, k, 1, own, c, d_yp).start()
+        ag_copy(w, k, 1, own, c, d_ym).start()
+
+    def ag_x(w, k):
+        ag_copy(w, k, 0, 2 * y + xn, c, d_xn).wait_recv()
+        at = 2 * y + xn if w == 0 and k < 2 else pair
+        ag_copy(w, k, 1, at, c, d_yp).start()
+        ag_copy(w, k, 1, at, c, d_ym).start()
+        ag_copy(w, k, 3, pair, c, d_sib).start()
+
+    def ag_y(w, k):
+        ag_copy(w, k, 1, pl.ds(0, 4), c, d_yp).wait_recv()
+        ag_copy(w, k, 2, 2 * ym, c, d_yp).start()
+        ag_copy(w, k, 2, 2 * yp + 1, c, d_ym).start()
+        ag_copy(w, k, 3, pair_m, c, d_sib).start()
+        ag_copy(w, k, 3, pair_p, c, d_sib).start()
+
+    def ag_far(w, k):
+        ag_copy(w, k, 2, pair_2, c, d_yp).wait_recv()
+        ag_copy(w, k, 3, pair_2, c, d_sib).start()
+
+    def ag_sib(w, k):
+        ag_copy(w, k, 3, slice(None), cn, d_sib).wait_recv()
 
     def ag_drain(w):
         for i, b in enumerate((bufs[w].at[:, own, c], bufs[w].at[:, pl.ds(0, 7)])):
@@ -158,24 +161,41 @@
     l_dout.wait()
     for o in range(4):
         buf_a[order[o], own, c] = own_dout[:, pl.ds(al(order[o] * 768, 128), 768)]
-        ag_sx(0, o)
-        if o < 2:
-            ag_sy(0, o)
-
-    l_tok.wait()
-    x = own_tok[...].astype(F32)
-    center = jnp.mean(x, axis=-1, keepdims=True)
-    spread = jnp.mean((x - center) ** 2, axis=-1, keepdims=True)
-    rstd = 1.0 / jnp.sqrt(spread + 1e-06)
-    xhat[...] = (x - center) * rstd
-    rstd_ref[...] = jnp.broadcast_to(rstd, rstd_ref.shape)
-    for o in range(4):
-        buf_b[o, own, c] = (
-            xhat[:, pl.ds(o * 768, 768)] * gain[:, pl.ds(o * 768, 768)]
-        ).astype(BF16)
-
-    for o in range(4):
-        ag_sx(1, o)
+    ag_sx(0, 0)
+    ag_sy(0, 0)
+    ag_sx(0, 1)
+    ag_sy(0, 1)
+    ag_sx(0, 2)
+    ag_sx(0, 3)
+    ag_sx(0, 4)
+
+    def layer_norm():
+        l_tok.wait()
+        l_gain.wait()
+        x = own_tok[...].astype(F32)
+        center = jnp.mean(x, axis=-1, keepdims=True)
+        spread = jnp.mean((x - center) ** 2, axis=-1, keepdims=True)
+        rstd = 1.0 / jnp.sqrt(spread + 1e-06)
+        xhat[...] = (x - center) * rstd
+        rstd_ref[...] = jnp.broadcast_to(rstd, rstd_ref.shape)
+        for o in range(4):
+            for half, dst in ((xh, buf_b.at[o, own, c, :, pl.ds(0, 384)]), (xo, nsend.at[o])):
+                cols = pl.ds(al(o * 768 + half * 384, 128), 384)
+                dst[...] = (xhat[:, cols] * gain[:, cols]).astype(BF16)
+            nx_copy(o).start()
+
+    def nx_copy(o):
+        dst = buf_b.at[o, own, c, :, pl.ds(384, 384)]
+        return remote(nsend.at[o], dst, nx_s.at[0], nx_s.at[1], d_xo)
+
+    def nx_all():
+        b = buf_b.at[:, own, c, :, pl.ds(384, 384)]
+        return remote(nsend, b, nx_s.at[0], nx_s.at[1], d_xo)
+
+    def nx_take():
+        nx_all().wait_recv()
+        for o in range(4):
+            ag_sx(1, o)
 
     def att_fwd(b):
         rows = pl.ds(b * 256, 256)
@@ -201,22 +221,26 @@
 
     l_pre.wait()
     gelu(0)
+    gelu(1)
     ag_x(0, 0)
     l_qkv.wait()
-    gelu(1)
+    att_fwd(0)
     ag_x(0, 1)
-    att_fwd(0)
     att_fwd(1)
+    ag_y(0, 0)
     att_fwd(2)
+    ag_x(0, 2)
     gelu(2)
-    ag_y(0, 0)
-    ag_x(0, 2)
+    ag_y(0, 1)
+    ag_x(0, 3)
     gelu(3)
     gelu(4)
     gelu(5)
-    ag_y(0, 1)
-    ag_x(0, 3)
     ag_far(0, 0)
+    layer_norm()
+    ag_y(0, 2)
+    ag_far(0, 1)
+    ag_x(0, 4)
     ag_sib(0, 0)
 
     class Ring:
@@ -236,6 +260,17 @@
         def far(self):
             self.send(0, self.src(z2, 1), d_zp)
             self.send(1, self.src(z2, 0), d_zm)
+
+        def far_block(self, h):
+            for i, d in ((0, d_zp), (1, d_zm)):
+                cp = remote(
+                    self.src(z2, 1 - i).at[h], self.rbuf.at[i, h],
+                    self.ssem.at[i], self.rsem.at[i], d,
+                )
+                cp.start()
+                if h == 0:
+                    b = self.rbuf.at[i]
+                    self.sent.append(remote(b, b, self.ssem.at[i], self.rsem.at[i], d))
 
         def near_p(self):
             self.send(2, self.src(zp, 0), d_zp)
@@ -286,13 +321,14 @@
         Ring(z_first(cout, s * 2 * HO, HO), rzo.at[s], zo_s.at[s], zo_r.at[s], adder(both, HO, 64))
         for s in range(NSO)
     ]
-    ri = [
-        Ring(z_first(cin, s * 2 * HI, HI), rzi.at[s], zi_s.at[s], zi_r.at[s], adder(both, HI, 16))
-        for s in range(NSI)
+    def in_src(n):
+        return lambda zz, half: cin.at[n, zz, pl.ds(half * 192, 192), :]
+
+    rn = [
+        Ring(in_src(n), rzi.at[n], zi_s.at[n], zi_r.at[n], adder(((),), 192, 96)) for n in range(6)
     ]
-    base_o, base_i = 1024 - XO, 384 - XI
+    base_o = 1024 - XO
     fo = Ring(x_first(cout, base_o, XO // 2), rfo, fo_s, fo_r, adder(((),), XO // 2, 64))
-    fi = Ring(x_first(cin, base_i, XI // 2), rfi, fi_s, fi_r, adder(((),), XI // 2, 16))
 
     class Cross:
         def __init__(self, ring, part, rx, ssem, rsem, base, height, tile):
@@ -402,11 +438,17 @@
     co = [
         Cross(ro[s], cout, rxo, xo_s.at[s], xo_r.at[s], s * 2 * HO, HO, 64) for s in range(NSO)
     ]
-    ci = [
-        Cross(ri[s], cin, rxi, xi_s.at[s], xi_r.at[s], s * 2 * HI, HI, 16) for s in range(NSI)
-    ]
     xfo = First(fo, cout, x1o, rxo, x1o_s, x1o_r, base_o, XO, 64)
-    xfi = First(fi, cin, x1i, rxi, x1i_s, x1i_r, base_i, XI, 16)
+
+    def out_half(h):
+        j = order[0]
+
+        def step(r):
+            rows = pl.ds(al(r * 256, 256), 256)
+            right_side = buf_a[j, :, :, :, pl.ds(h * 384, 384)].reshape(768, 384)
+            cout[j * 2 + h, rows, :] = nn(joined_t[rows, :], right_side).astype(BF16)
+
+        loop(4, step)
 
     def out_chunk(o):
         j = order[o]
@@ -419,34 +461,39 @@
 
         loop(4, step)
 
-    out_chunk(0)
+    out_half(0)
     for r in ro:
-        r.far()
+        r.far_block(0)
+    ag_sib(0, 1)
+    out_half(1)
+    for r in ro:
+        r.far_block(1)
+    nx_take()
     xfo.send(0)
-    ag_far(0, 1)
-    ag_y(0, 2)
-    ag_sib(0, 1)
+    ag_far(0, 2)
+    ag_y(0, 3)
+    ag_sib(0, 2)
     out_chunk(1)
     for r in ro:
         r.near_p()
     xfo.send(1)
-    ag_far(0, 2)
-    ag_y(0, 3)
+    ag_far(0, 3)
+    ag_y(0, 4)
     ag_x(1, 0)
-    ag_x(1, 1)
-    ag_sib(0, 2)
+    ag_sib(0, 3)
     out_chunk(2)
     for r in ro:
         r.near_m()
     xfo.send(2)
-    ag_far(0, 3)
+    ag_far(0, 4)
+    ag_x(1, 1)
+    ag_sib(0, 4)
+    out_chunk(3)
+    xfo.send(3)
+    ag_y(1, 0)
     ro[0].relay_p()
     ro[0].relay_m()
-    ag_y(1, 0)
     ag_x(1, 2)
-    ag_sib(0, 3)
-    out_chunk(3)
-    xfo.send(3)
     ag_y(1, 1)
     ag_x(1, 3)
     ag_far(1, 0)
@@ -469,23 +516,35 @@
                 gh[rows, :] = g
             else:
                 cols = pl.ds((nb - 1) * 256, 256)
-                gproj[rows, pl.ds(768 + (nb - 1) * 256, 256)] = (
-                    g.astype(F32) * slope[rows, cols]
-                ).astype(BF16)
+                gproj[2 + nb, rows, :] = (g.astype(F32) * slope[rows, cols]).astype(BF16)
 
         loop(2, step)
 
-    joined_grad(0)
-    for l in wo_loads[3]:
+    def gx_copy(n):
+        return remote(gproj.at[n], gp2.at[n], gx_s, gx_r.at[n], d_xo)
+
+    def gx_send(n):
+        gx_copy(n).start()
+
+    def gx_wait(n):
+        gx_copy(n).wait_recv()
+
+    joined_grad(1)
+    gx_send(3)
+    for l in wo_loads[0]:
         l.start()
-    joined_grad(1)
     ag_far(1, 1)
     ag_y(1, 2)
+    joined_grad(2)
+    gx_send(4)
     xfo.take(0)
-    joined_grad(2)
     joined_grad(3)
+    gx_send(5)
     ag_far(1, 2)
     ag_y(1, 3)
+    ro[2].relay_p()
+    ro[2].relay_m()
+    joined_grad(0)
 
     def win_load(j):
         return load(
@@ -508,13 +567,17 @@
                 axis=-1, keepdims=True,
             )
             ds = (p * (nt(g, v) - delta) * SCALE).astype(BF16)
-            gproj[rows, pl.ds(512 + h * 128, 128)] = tn(p.astype(BF16), g).astype(BF16)
-            gproj[rows, pl.ds(h * 128, 128)] = nn(ds, k).astype(BF16)
-            gproj[rows, pl.ds(256 + h * 128, 128)] = tn(ds, q).astype(BF16)
+            gproj[2, rows, pl.ds(h * 128, 128)] = tn(p.astype(BF16), g).astype(BF16)
+            gproj[0, rows, pl.ds(h * 128, 128)] = nn(ds, k).astype(BF16)
+            gproj[1, rows, pl.ds(h * 128, 128)] = tn(ds, q).astype(BF16)
 
     att_bwd(0)
     att_bwd(1)
     att_bwd(2)
+    gx_send(2)
+    gx_send(0)
+    gx_send(1)
+    ag_far(1, 3)
     xfo.take(1)
 
     ag_drain(0)
@@ -530,37 +593,36 @@
 
         loop(2, step)
 
-    def in_chunk(o):
+    def in_block(n, o):
         j = order[o]
-
-        def step(i):
-            h, n = i // 2, i % 2
-            cols = pl.ds(al(n * 768, 128), 768)
-            left_side = buf_a[j, pl.ds(h * 4, 4)].reshape(384, 768)
-            cin[j * 2 + h, :, cols] = nn(left_side, gproj[:, cols]).astype(BF16)
-
-        loop(4, step)
+        left_own = buf_a[j, pl.ds(0, 4)].reshape(384, 768)
+        left_other = buf_a[j, pl.ds(4, 4)].reshape(384, 768)
+        cin[n, j] = (nn(left_own, gproj[n]) + nn(left_other, gp2[n])).astype(BF16)
+
+    def in_finish(n):
+        rn[n].arrived()
+        r = rzi.at[n]
+        for half, (a, b) in enumerate(((2, 5), (3, 4))):
+            rows = pl.ds(half * 192, 192)
+            rxi[n, rows, :] = (
+                r[a].astype(F32) + r[b].astype(F32) + cin[n, z, rows, :].astype(F32)
+            ).astype(BF16)
 
     transposed(0)
-    in_chunk(0)
-    for r in ri:
-        r.far()
-    xfi.send(0)
-    ag_far(1, 3)
     transposed(1)
-    in_chunk(1)
-    ri[0].near_p()
-    xfi.send(1)
+    transposed(2)
+    transposed(3)
+    ag_drain(1)
+    gx_wait(3)
+    in_block(3, 0)
+    rn[3].far()
+    in_block(3, 1)
+    rn[3].near_p()
+    in_block(3, 2)
+    rn[3].near_m()
+    in_block(3, 3)
     xfo.take(2)
-    transposed(2)
-    in_chunk(2)
-    ri[0].near_m()
-    xfi.send(2)
-    transposed(3)
-    in_chunk(3)
-    xfi.send(3)
     xfo.take(3)
-    ag_drain(1)
 
     def sib_copy(j):
         return remote(buf_b.at[j, :, cn], rs_sib.at[j], m_s.at[0], ms_r.at[j], d_sib)
@@ -573,7 +635,10 @@
             h, n = i // 3, i % 3
             rows = pl.ds(al(h * 384, 128), 384)
             w = wslot[pl.ds(al(base + n * 256, 256), 256), :]
-            t = nt(gproj[rows, :], w).astype(BF16)
+            acc = nt(gproj[0, rows, :], w[:, :256])
+            for k in range(1, 6):
+                acc = acc + nt(gproj[k, rows, :], w[:, k * 256 : k * 256 + 256])
+            t = acc.astype(BF16)
             cols = pl.ds(al(n * 256, 128), 256)
             buf_b[j, pl.ds(h * 4, 4), :, :, cols] = t.reshape(4, 2, 48, 256)
 
@@ -616,38 +681,85 @@
         gn[:, cols] = gn[:, cols] + rs_x[j].astype(F32)
 
     normed_grad(0)
-    ri[0].relay_p()
-    ri[0].relay_m()
-    ri[1].near_p()
-    ri[1].near_m()
+    gx_wait(4)
+    in_block(4, 0)
+    rn[4].far()
+    in_block(4, 1)
+    rn[4].near_p()
+    in_block(4, 2)
+    rn[4].near_m()
+    in_block(4, 3)
+    rn[3].relay_p()
+    rn[3].relay_m()
     normed_grad(1)
     sib_sum(0)
+    fo.relay_p()
+    fo.relay_m()
+    gx_wait(5)
+    in_block(5, 0)
+    rn[5].far()
+    in_block(5, 1)
+    rn[5].near_p()
+    in_block(5, 2)
+    rn[5].near_m()
+    in_block(5, 3)
+    rn[4].relay_p()
+    rn[4].relay_m()
+    normed_grad(2)
+    sib_sum(1)
     co[0].send()
     co[1].send()
-    normed_grad(2)
-    ri[1].relay_p()
-    ri[1].relay_m()
-    ri[2].near_p()
-    ri[2].near_m()
-    sib_sum(1)
+    y_sum(0)
+    gx_wait(2)
+    in_block(2, 0)
+    rn[2].far()
+    in_block(2, 1)
+    rn[2].near_p()
+    in_block(2, 2)
+    rn[2].near_m()
+    in_block(2, 3)
+    rn[5].relay_p()
+    rn[5].relay_m()
     normed_grad(3)
-    ri[2].relay_p()
-    ri[2].relay_m()
-    fo.relay_p()
-    fo.relay_m()
     sib_sum(2)
-    xfi.take(0)
+    y_sum(1)
+    co[2].send()
+    in_finish(3)
+    gx_wait(0)
+    in_block(0, 0)
+    rn[0].far()
+    in_block(0, 1)
+    rn[0].near_p()
+    in_block(0, 2)
+    rn[0].near_m()
+    in_block(0, 3)
+    rn[2].relay_p()
+    rn[2].relay_m()
     sib_sum(3)
-    y_sum(0)
-    xfi.take(1)
-    y_sum(1)
-    xfi.take(2)
     y_sum(2)
+    in_finish(4)
+    xfo.finish()
     y_sum(3)
-    xfi.take(3)
+    gx_wait(1)
+    in_block(1, 0)
+    rn[1].far()
+    in_block(1, 1)
+    rn[1].near_p()
+    in_block(1, 2)
+    rn[1].near_m()
+    in_block(1, 3)
+    rn[0].relay_p()
+    rn[0].relay_m()
+    in_finish(5)
+    rn[1].relay_p()
+    rn[1].relay_m()
+    in_finish(2)
     co[0].finish()
     co[1].finish()
-    ci[0].send()
+    co[2].finish()
+    st_o = load(rxo, gwout, 1)
+    st_o.start()
+    in_finish(0)
     for j in range(4):
         x_sum(j)
     xh_v = xhat[...]
@@ -659,25 +771,14 @@
     ).astype(BF16)
     st_g = load(own_tok, ig, 0)
     st_g.start()
-    ci[1].send()
-    ci[0].finish()
-    ci[1].finish()
-    ci[2].send()
-    xfo.finish()
-    st_o = load(rxo, gwout, 1)
-    st_o.start()
-    fi.relay_p()
-    fi.relay_m()
-    st_i = [
-        load(rxi.at[pl.ds(a, n)], gwin.at[pl.ds(a, n)], 2 + i)
-        for i, (a, n) in enumerate(((0, 4 * HI), (4 * HI, 2 * HI), (base_i, XI)))
-    ]
-    st_i[0].start()
-    xfi.finish()
-    st_i[2].start()
-    ci[2].finish()
-    st_i[1].start()
-    for r in ro + ri + [fo, fi] + co + ci + [xfo, xfi]:
+    in_finish(1)
+    st_i = [load(rxi.at[n], gwin.at[:, pl.ds(n * 256, 256)], 2 + n) for n in range(6)]
+    for st in st_i:
+        st.start()
+    gx_all = remote(gproj, gp2, gx_s, gx_r.at[0], d_xo)
+    gx_all.wait_send()
+    nx_all().wait_send()
+    for r in ro + rn + [fo] + co + [xfo]:
         r.drain()
     for b, i in ((rs_sib, 0), (rs_y, 1), (rs_x, 2)):
         remote(b, b, m_s.at[i], mx_r.at[0], d_sib).wait_send()
@@ -685,6 +786,30 @@
     st_g.wait()
     for st in st_i:
         st.wait()
+
+
+def widen(ig, gwin, gwout, ig_out, gwin_out, gwout_out, tg, ti, to, fi, fo, isem, osem):
+    def copies(k):
+        if k == 8:
+            return ig, tg, tg, ig_out
+        if k < 4:
+            at = pl.ds(k * 96, 96)
+            return gwin.at[at], ti.at[at], fi.at[at], gwin_out.at[at]
+        at = pl.ds((k - 4) * 256, 256)
+        return gwout.at[at], to.at[at], fo.at[at], gwout_out.at[at]
+
+    ins = [pltpu.make_async_copy(copies(k)[0], copies(k)[1], isem.at[k]) for k in range(9)]
+    outs = [pltpu.make_async_copy(copies(k)[2], copies(k)[3], osem.at[k]) for k in range(9)]
+    for cp in ins:
+        cp.start()
+    for k in range(9):
+        ins[k].wait()
+        if k < 8:
+            src, dst = copies(k)[1:3]
+            dst[...] = src[...].astype(F32)
+        outs[k].start()
+    for cp in outs:
+        cp.wait()
 
 
 def body(block_input_tokens, norm_gain_vector, w_in, w_out, saved_qkv, mlp_pre, output_gradient):
@@ -699,26 +824,25 @@
             jax.ShapeDtypeStruct((384, 1536), BF16),
             jax.ShapeDtypeStruct((1024, 384), BF16),
         ),
-        in_specs=[hbm, pl.BlockSpec(memory_space=pltpu.VMEM), hbm, hbm, hbm, hbm, hbm],
+        in_specs=[hbm] * 7,
         out_specs=(hbm, hbm, hbm),
         scratch_shapes=[
             v((4, 8, 2, 48, 768), BF16), v((4, 8, 2, 48, 768), BF16), v((768, 768), BF16),
             v((768, 768), BF16), v((768, 768), F32), v((6, 256, 256), F32),
             v((768, 256), BF16), v((1024, 768), BF16), v((768, 256), BF16),
-            v((768, 1536), BF16), v((1536, 1536), BF16), v((8, 1024, 384), BF16),
-            v((8, 384, 1536), BF16),
-            v((NSO, 6, 2, HO, 384), BF16), v((NSI, 6, 2, HI, 1536), BF16),
-            v((6, XO // 2, 384), BF16), v((6, XI // 2, 1536), BF16),
-            v((4, XO, 384), BF16), v((4, XI, 1536), BF16),
-            v((1024, 384), BF16), v((384, 1536), BF16), v((4, 8, 48, 768), BF16),
+            v((6, 768, 256), BF16), v((6, 768, 256), BF16), v((1536, 1536), BF16),
+            v((8, 1024, 384), BF16), v((6, 4, 384, 256), BF16),
+            v((NSO, 6, 2, HO, 384), BF16), v((6, 6, 192, 256), BF16),
+            v((6, XO // 2, 384), BF16), v((4, XO, 384), BF16),
+            v((1024, 384), BF16), v((6, 384, 256), BF16), v((4, 48, 384), BF16),
+            v((4, 8, 48, 768), BF16),
             v((4, 3, 2, 48, 768), BF16), v((4, 48, 768), BF16), v((4, 48, 768), BF16),
-            v((48, 3072), F32), v((48, 3072), F32), v((48, 3072), BF16),
+            v((48, 3072), F32), v((48, 3072), F32), v((1, 3072), F32), v((48, 3072), BF16),
             v((48, 3072), BF16), v((48, 128), F32),
-            sem((16,)), sem((2, 2)), sem((2, 4, 4)),
-            sem((NSO, 6)), sem((NSO, 6)), sem((NSI, 6)), sem((NSI, 6)),
-            sem((6,)), sem((6,)), sem((6,)), sem((6,)),
-            sem((NSO, 2)), sem((NSO, 2)), sem((NSI, 2)), sem((NSI, 2)),
-            sem((4,)), sem((4,)), sem((4,)), sem((4,)), sem((3,)), sem((4,)), sem((4,)), sem((4,)),
+            sem((16,)), sem((2, 2)), sem((2, 5, 4)),
+            sem((NSO, 6)), sem((NSO, 6)), sem((6, 6)), sem((6, 6)), sem((6,)), sem((6,)),
+            sem((NSO, 2)), sem((NSO, 2)),
+            sem((4,)), sem((4,)), sem, sem((6,)), sem((2,)), sem((3,)), sem((4,)), sem((4,)), sem((4,)),
         ],
         compiler_params=pltpu.CompilerParams(
             collective_id=0, has_side_effects=True, vmem_limit_bytes=63 << 20
@@ -727,7 +851,22 @@
         block_input_tokens, norm_gain_vector.reshape(1, -1), w_in, w_out, saved_qkv, mlp_pre,
         output_gradient,
     )
-    return ig, gwin.astype(F32), gwout.astype(F32)
+    return pl.pallas_call(
+        widen,
+        name="widen",
+        out_shape=(
+            jax.ShapeDtypeStruct((48, 3072), BF16),
+            jax.ShapeDtypeStruct((384, 1536), F32),
+            jax.ShapeDtypeStruct((1024, 384), F32),
+        ),
+        in_specs=[hbm] * 3,
+        out_specs=(hbm,) * 3,
+        scratch_shapes=[
+            v((48, 3072), BF16), v((384, 1536), BF16), v((1024, 384), BF16),
+            v((384, 1536), F32), v((1024, 384), F32), sem((9,)), sem((9,)),
+        ],
+        compiler_params=pltpu.CompilerParams(vmem_limit_bytes=62 << 20),
+    )(ig, gwin, gwout)
 
 
 def solution(mesh):

time: 139 us -> 125 us (0.90)
  Pallas kernels: 132 us -> 124 us
  other arithmetic: 4.28 us -> 0 us
    pallas_call x1, Pallas kernels: 132 us -> 121 us  [body(): pl.pallas_call(kernel, name='block_backward', out_shape=(jax.ShapeDtypeSt...]
    convert_element_type x2 -> x0, other arithmetic: 4.28 us -> none  [body(): return (ig, gwin.astype(F32), gwout.astype(F32))]
    pallas_call x0 -> x1, Pallas kernels: none -> 3.17 us  [body(): pl.pallas_call(widen, name='widen', out_shape=(jax.ShapeDtypeStruct((48,...]
where the time goes in v4:
time: 125 us
  Pallas kernels  124 us (99%)
    pallas_call x1, Pallas kernels, body(): pl.pallas_call(kernel, name='block_backward', out_shape=(jax.ShapeDtypeSt...  121 us
    pallas_call x1, Pallas kernels, body(): pl.pallas_call(widen, name='widen', out_shape=(jax.ShapeDtypeStruct((48,...  3.17 us

profile of v4, /device:TPU:0, one launch (start us, length us, event | category | flops | bytes accessed | tf_op | source)
XLA Modules:
  0.0 124.6 jit_solution(6133367888388577922)
XLA Ops:
  0.6 120.6 %block_backward.1 = (bf16[48,3072]{1,0:T(8,128)(2,1)}, bf16[384,1536]{1,0:T(8,128)(2,1)}, bf16[1024,384]{1,0:T(8,128)(2,1)}) custom-call(bf16[48,3072]{1,0:T(8,128)(2,1)} %tok.1, f32[1,3072]{1,0:T(1,128)} %bitcast.1, bf16[3072,1536]{1,0:T(8,128)(2,1)} %win.1, bf16[1024,3072]{1,0:T(8,128)(2,1)} %wout.1, bf16[768,768]{1,0:T(8,128)(2,1)} %qkv_hbm.1, ...), custom_call_target="tpu_custom_call" | custom-call | tf_op jit(solution)/shard_map/block_backward/pallas_call | solution.py:819
  121.3 3.2 %widen.1 = (bf16[48,3072]{1,0:T(8,128)(2,1)}, f32[384,1536]{1,0:T(8,128)}, f32[1024,384]{1,0:T(8,128)}) custom-call(bf16[48,3072]{1,0:T(8,128)(2,1)} %get-tuple-element.6.ig, bf16[384,1536]{1,0:T(8,128)(2,1)} %get-tuple-element.7.gwin, bf16[1024,384]{1,0:T(8,128)(2,1)} %get-tuple-element.8.gwout), custom_call_target="tpu_custom_call" | custom-call | tf_op jit(solution)/shard_map/widen/pallas_call | solution.py:854

commit v5 on v4

--- a/solution.py
+++ b/solution.py
@@ -12,7 +12,7 @@
 BF16 = jnp.bfloat16
 SCALE = HD ** (-0.5)
 MESH = pl.DeviceIdType.MESH
-NSO, HO, XO = 3, 128, 256
+NSO, HO, XO = 3, 144, 160
 BLOCKS = (3, 4, 5, 2, 0, 1)
 
 
@@ -233,11 +233,11 @@
     gelu(2)
     ag_y(0, 1)
     ag_x(0, 3)
+    layer_norm()
     gelu(3)
     gelu(4)
     gelu(5)
     ag_far(0, 0)
-    layer_norm()
     ag_y(0, 2)
     ag_far(0, 1)
     ag_x(0, 4)
@@ -318,7 +318,7 @@
 
     both = ((0,), (1,))
     ro = [
-        Ring(z_first(cout, s * 2 * HO, HO), rzo.at[s], zo_s.at[s], zo_r.at[s], adder(both, HO, 64))
+        Ring(z_first(cout, s * 2 * HO, HO), rzo.at[s], zo_s.at[s], zo_r.at[s], adder(both, HO, 48))
         for s in range(NSO)
     ]
     def in_src(n):
@@ -328,7 +328,7 @@
         Ring(in_src(n), rzi.at[n], zi_s.at[n], zi_r.at[n], adder(((),), 192, 96)) for n in range(6)
     ]
     base_o = 1024 - XO
-    fo = Ring(x_first(cout, base_o, XO // 2), rfo, fo_s, fo_r, adder(((),), XO // 2, 64))
+    fo = Ring(x_first(cout, base_o, XO // 2), rfo, fo_s, fo_r, adder(((),), XO // 2, 16))
 
     class Cross:
         def __init__(self, ring, part, rx, ssem, rsem, base, height, tile):
@@ -436,9 +436,9 @@
                 self.copy(o).wait_send()
 
     co = [
-        Cross(ro[s], cout, rxo, xo_s.at[s], xo_r.at[s], s * 2 * HO, HO, 64) for s in range(NSO)
+        Cross(ro[s], cout, rxo, xo_s.at[s], xo_r.at[s], s * 2 * HO, HO, 48) for s in range(NSO)
     ]
-    xfo = First(fo, cout, x1o, rxo, x1o_s, x1o_r, base_o, XO, 64)
+    xfo = First(fo, cout, x1o, rxo, x1o_s, x1o_r, base_o, XO, 16)
 
     def out_half(h):
         j = order[0]
@@ -464,11 +464,11 @@
     out_half(0)
     for r in ro:
         r.far_block(0)
+    nx_take()
     ag_sib(0, 1)
     out_half(1)
     for r in ro:
         r.far_block(1)
-    nx_take()
     xfo.send(0)
     ag_far(0, 2)
     ag_y(0, 3)
@@ -488,17 +488,7 @@
     ag_far(0, 4)
     ag_x(1, 1)
     ag_sib(0, 4)
-    out_chunk(3)
-    xfo.send(3)
     ag_y(1, 0)
-    ro[0].relay_p()
-    ro[0].relay_m()
-    ag_x(1, 2)
-    ag_y(1, 1)
-    ag_x(1, 3)
-    ag_far(1, 0)
-    ro[1].relay_p()
-    ro[1].relay_m()
 
     def joined_grad(nb):
         for l in wo_loads[nb]:
@@ -533,18 +523,28 @@
     gx_send(3)
     for l in wo_loads[0]:
         l.start()
+    ag_x(1, 2)
+    ag_y(1, 1)
+    out_chunk(3)
+    xfo.send(3)
+    ag_x(1, 3)
+    ag_far(1, 0)
+    ro[0].relay_p()
+    ro[0].relay_m()
+    joined_grad(2)
+    gx_send(4)
     ag_far(1, 1)
     ag_y(1, 2)
-    joined_grad(2)
-    gx_send(4)
     xfo.take(0)
     joined_grad(3)
     gx_send(5)
+    ro[1].relay_p()
+    ro[1].relay_m()
     ag_far(1, 2)
     ag_y(1, 3)
+    joined_grad(0)
     ro[2].relay_p()
     ro[2].relay_m()
-    joined_grad(0)
 
     def win_load(j):
         return load(
@@ -689,8 +689,6 @@
     in_block(4, 2)
     rn[4].near_m()
     in_block(4, 3)
-    rn[3].relay_p()
-    rn[3].relay_m()
     normed_grad(1)
     sib_sum(0)
     fo.relay_p()
@@ -703,13 +701,14 @@
     in_block(5, 2)
     rn[5].near_m()
     in_block(5, 3)
+    rn[3].relay_p()
+    rn[3].relay_m()
+    normed_grad(2)
+    sib_sum(1)
     rn[4].relay_p()
     rn[4].relay_m()
-    normed_grad(2)
-    sib_sum(1)
     co[0].send()
     co[1].send()
-    y_sum(0)
     gx_wait(2)
     in_block(2, 0)
     rn[2].far()
@@ -718,13 +717,12 @@
     in_block(2, 2)
     rn[2].near_m()
     in_block(2, 3)
+    normed_grad(3)
+    sib_sum(2)
+    y_sum(0)
     rn[5].relay_p()
     rn[5].relay_m()
-    normed_grad(3)
-    sib_sum(2)
-    y_sum(1)
     co[2].send()
-    in_finish(3)
     gx_wait(0)
     in_block(0, 0)
     rn[0].far()
@@ -733,13 +731,13 @@
     in_block(0, 2)
     rn[0].near_m()
     in_block(0, 3)
+    sib_sum(3)
+    y_sum(1)
     rn[2].relay_p()
     rn[2].relay_m()
-    sib_sum(3)
-    y_sum(2)
+    in_finish(3)
     in_finish(4)
     xfo.finish()
-    y_sum(3)
     gx_wait(1)
     in_block(1, 0)
     rn[1].far()
@@ -750,16 +748,19 @@
     in_block(1, 3)
     rn[0].relay_p()
     rn[0].relay_m()
+    y_sum(2)
+    y_sum(3)
     in_finish(5)
     rn[1].relay_p()
     rn[1].relay_m()
     in_finish(2)
+    in_finish(0)
     co[0].finish()
     co[1].finish()
     co[2].finish()
     st_o = load(rxo, gwout, 1)
     st_o.start()
-    in_finish(0)
+    in_finish(1)
     for j in range(4):
         x_sum(j)
     xh_v = xhat[...]
@@ -771,7 +772,6 @@
     ).astype(BF16)
     st_g = load(own_tok, ig, 0)
     st_g.start()
-    in_finish(1)
     st_i = [load(rxi.at[n], gwin.at[:, pl.ds(n * 256, 256)], 2 + n) for n in range(6)]
     for st in st_i:
         st.start()

time: 125 us -> 119 us (0.952)
  Pallas kernels: 124 us -> 118 us
    pallas_call x1, Pallas kernels: 121 us -> 115 us  [body(): pl.pallas_call(kernel, name='block_backward', out_shape=(jax.ShapeDtypeSt...]
where the time goes in v5:
time: 119 us
  Pallas kernels  118 us (99%)
    pallas_call x1, Pallas kernels, body(): pl.pallas_call(kernel, name='block_backward', out_shape=(jax.ShapeDtypeSt...  115 us
    pallas_call x1, Pallas kernels, body(): pl.pallas_call(widen, name='widen', out_shape=(jax.ShapeDtypeStruct((48,...  3.17 us

profile of v5, /device:TPU:0, one launch (start us, length us, event | category | flops | bytes accessed | tf_op | source)
XLA Modules:
  0.0 118.9 jit_solution(5393818897622183262)
XLA Ops:
  0.6 114.9 %block_backward.1 = (bf16[48,3072]{1,0:T(8,128)(2,1)}, bf16[384,1536]{1,0:T(8,128)(2,1)}, bf16[1024,384]{1,0:T(8,128)(2,1)}) custom-call(bf16[48,3072]{1,0:T(8,128)(2,1)} %tok.1, f32[1,3072]{1,0:T(1,128)} %bitcast.1, bf16[3072,1536]{1,0:T(8,128)(2,1)} %win.1, bf16[1024,3072]{1,0:T(8,128)(2,1)} %wout.1, bf16[768,768]{1,0:T(8,128)(2,1)} %qkv_hbm.1, ...), custom_call_target="tpu_custom_call" | custom-call | tf_op jit(solution)/shard_map/block_backward/pallas_call | solution.py:819
  115.5 3.2 %widen.1 = (bf16[48,3072]{1,0:T(8,128)(2,1)}, f32[384,1536]{1,0:T(8,128)}, f32[1024,384]{1,0:T(8,128)}) custom-call(bf16[48,3072]{1,0:T(8,128)(2,1)} %get-tuple-element.6.ig, bf16[384,1536]{1,0:T(8,128)(2,1)} %get-tuple-element.7.gwin, bf16[1024,384]{1,0:T(8,128)(2,1)} %get-tuple-element.8.gwout), custom_call_target="tpu_custom_call" | custom-call | tf_op jit(solution)/shard_map/widen/pallas_call | solution.py:854

commit v6 on v5

--- a/solution.py
+++ b/solution.py
@@ -761,6 +761,9 @@
     st_o = load(rxo, gwout, 1)
     st_o.start()
     in_finish(1)
+    st_i = [load(rxi.at[n], gwin.at[:, pl.ds(n * 256, 256)], 2 + n) for n in range(6)]
+    for st in st_i:
+        st.start()
     for j in range(4):
         x_sum(j)
     xh_v = xhat[...]
@@ -772,9 +775,6 @@
     ).astype(BF16)
     st_g = load(own_tok, ig, 0)
     st_g.start()
-    st_i = [load(rxi.at[n], gwin.at[:, pl.ds(n * 256, 256)], 2 + n) for n in range(6)]
-    for st in st_i:
-        st.start()
     gx_all = remote(gproj, gp2, gx_s, gx_r.at[0], d_xo)
     gx_all.wait_send()
     nx_all().wait_send()

time: 119 us -> 119 us (level)
  no operation moved by 1% of the time
where the time goes in v6:
time: 119 us; the launch traced here: 118 us
  Pallas kernels  118 us (99%)
    pallas_call x1, Pallas kernels, body(): pl.pallas_call(kernel, name='block_backward', out_shape=(jax.ShapeDtypeSt...  114 us
    pallas_call x1, Pallas kernels, body(): pl.pallas_call(widen, name='widen', out_shape=(jax.ShapeDtypeStruct((48,...  3.17 us

profile of v6, /device:TPU:0, one launch (start us, length us, event | category | flops | bytes accessed | tf_op | source)
XLA Modules:
  0.0 118.5 jit_solution(7541444526297799815)
XLA Ops:
  0.6 114.5 %block_backward.1 = (bf16[48,3072]{1,0:T(8,128)(2,1)}, bf16[384,1536]{1,0:T(8,128)(2,1)}, bf16[1024,384]{1,0:T(8,128)(2,1)}) custom-call(bf16[48,3072]{1,0:T(8,128)(2,1)} %tok.1, f32[1,3072]{1,0:T(1,128)} %bitcast.1, bf16[3072,1536]{1,0:T(8,128)(2,1)} %win.1, bf16[1024,3072]{1,0:T(8,128)(2,1)} %wout.1, bf16[768,768]{1,0:T(8,128)(2,1)} %qkv_hbm.1, ...), custom_call_target="tpu_custom_call" | custom-call | tf_op jit(solution)/shard_map/block_backward/pallas_call | solution.py:819
  115.1 3.2 %widen.1 = (bf16[48,3072]{1,0:T(8,128)(2,1)}, f32[384,1536]{1,0:T(8,128)}, f32[1024,384]{1,0:T(8,128)}) custom-call(bf16[48,3072]{1,0:T(8,128)(2,1)} %get-tuple-element.6.ig, bf16[384,1536]{1,0:T(8,128)(2,1)} %get-tuple-element.7.gwin, bf16[1024,384]{1,0:T(8,128)(2,1)} %get-tuple-element.8.gwout), custom_call_target="tpu_custom_call" | custom-call | tf_op jit(solution)/shard_map/widen/pallas_call | solution.py:854
